TPU v7x, 256 devices: a whole 4x4x8 slice. The times are simulated.
256 devices in a mesh: group: 4 (over x), bulk: 64 (over y, z, core).
Axes of the slice: x: 4, y: 4, z: 8, core: 2. Of those that a mesh axis runs over, the one named last changes fastest.
Arguments:
- right_sides: float32 [32, 524288], P(None, ('group', 'bulk')), may hold values from -6 to 6
- points: float32 [3, 524288], P(None, ('group', 'bulk')), may hold values from 0 to 4
- basis: float32 [2048, 64, 256], P(('group', 'bulk')), may hold values from -0.375 to 0.375
- transfer: float32 [3840, 64, 64], P(('group', 'bulk')), may hold values from -0.5 to 0.5
- skeleton: float32 [3840, 3, 64], P(('group', 'bulk')), may hold values from 0 to 2
- near_list: int32 [2048, 8], P(('group', 'bulk')), may hold values from 0 to 2047, as said below
- near_count: int32 [2048], P(('group', 'bulk')), may hold values from 0 to 8
- inter_list: int32 [3840, 8], P(('group', 'bulk')), may hold values from 0 to 2047, as said below
- inter_count: int32 [3840], P(('group', 'bulk')), may hold values from 0 to 8
- upper_transfer: float32 [256, 64, 64], replicated, may hold values from -0.5 to 0.5
- upper_skeleton: float32 [256, 3, 64], replicated, may hold values from 0 to 2
- upper_list: int32 [256, 8], replicated, may hold values from 0 to 255, as said below
- upper_count: int32 [256], replicated, may hold values from 0 to 8, as said below
Outputs:
- product: float32 [32, 524288], P(None, ('group', 'bulk'))
Inputs may be any that keep to these rules, and one draw needn't show every extreme that they name: `near_list`: row t holds distinct leaves other than t at most 4 leaves away; only the first near_count[t] entries count, the rest are in range and are ignored. `inter_list`: A node's row holds distinct other nodes of its level, each of the first inter_count entries at most max(m // 2, 1) places away where m is the level's nodes on one device; only the first inter_count entries count, the rest are in range and are ignored. `upper_list`: row h holds distinct other heap nodes of h's level; at levels with more nodes than there are indices of group, they lie below the same ancestor at the level that has one node per index of group. Only the first upper_count entries count, the rest are in range and are ignored. `upper_count`: entries 0 and 1 are 0.
All inputs are finite; a program needn't handle non-finite values.
Results may differ from a plain program's by a relative error of at most 0.0003.
Values sent between devices are 32-bit elements; how exact they have to be, the bound alone decides.
A program may use at most 128 MiB of HBM per device.

v0:
```python
import functools
import math

import jax
import jax.numpy as jnp
from jax import lax
from jax.experimental import pallas as pl
from jax.experimental.pallas import tpu as pltpu
from jax.sharding import PartitionSpec as P

F32 = jnp.float32
BF16 = jnp.bfloat16
MESH = pl.DeviceIdType.MESH
NN = (((1,), (0,)), ((), ()))
NT = (((1,), (1,)), ((), ()))

ALPHA = 2.0 / math.log(2.0)
KAPPA = 0.2 * math.log(2.0)
SHIFT = 1.0 / math.log(2.0)
SOFT = 0.01 * ALPHA * ALPHA
CENTER = 2.0
NUGGET = 0.5
FEATS = 48
UPPER = (32, 16, 8, 4, 2, 4, 2)
UPPER_AT = (0, 32, 48, 56, 60, 62, 66)


def dot(a, b, dims=NN):
    return lax.dot_general(a, b, dims, preferred_element_type=F32)


def halves(x):
    high = x.astype(BF16)
    return high, (x - high.astype(F32)).astype(BF16)


def matmul(a, high, low, dims=NN):
    m = a.shape[0]
    a_high, a_low = halves(a)
    both = dot(jnp.concatenate([a_high, a_low], axis=0), high, dims)
    return both[:m] + both[m:] + dot(a_high, low, dims)


def kern(w):
    y = w * lax.rsqrt(w)
    return halves((SHIFT + y) * jnp.exp2(-y))


def in_three(x):
    one = x.astype(BF16).astype(F32)
    rest = x - one
    two = rest.astype(BF16).astype(F32)
    return one, two, (rest - two).astype(BF16).astype(F32)


def scaled(x):
    return ALPHA * (x - CENTER)


def features(u, sides="st"):
    row = lax.broadcasted_iota(jnp.int32, u.shape, 0)
    square = jnp.sum(u * u, axis=0, keepdims=True)
    out = []
    if "s" in sides:
        s = jnp.where(row < 3, -2.0 * u, jnp.where(row == 3, square, jnp.where(row == 4, 1.0, 0.0)))
        a, b, c = in_three(s)
        out.append(jnp.concatenate([a, a, b, b, a, c], axis=0))
    if "t" in sides:
        t = jnp.where(row < 3, u, jnp.where(row == 3, 1.0, jnp.where(row == 4, square + SOFT, 0.0)))
        a, b, c = in_three(t)
        out.append(jnp.concatenate([a, b, a, b, c, a], axis=0).astype(BF16))
    return out


def as_rows(f):
    return f.T.astype(BF16)


def usable(values, counts):
    slot = lax.broadcasted_iota(jnp.int32, values.shape, 1)
    return jnp.where(slot < counts, values, -1000)


def counted(ref, rows, width):
    row = lax.broadcasted_iota(jnp.int32, (rows, width), 0)
    out = jnp.zeros((rows, width), jnp.int32)
    for t in range(rows):
        out = jnp.where(row == t, ref[t], out)
    return out


def mask(lists, ids):
    out = jnp.zeros((lists.shape[0], ids.shape[1]), F32)
    for i in range(lists.shape[1]):
        out += jnp.where(lists[:, i : i + 1] == ids, 1.0, 0.0)
    return out


def lanes(n):
    return lax.broadcasted_iota(jnp.int32, (1, n), 1)


def low_lanes(rows):
    return lax.broadcasted_iota(jnp.int32, (rows, 128), 1) < 64


def couple(rows, feats, coefs, masks):
    kh, kl = kern(dot(rows, feats))
    weighted = [coefs * (m * KAPPA) for m in masks]
    weighted = weighted[0] if len(weighted) == 1 else jnp.concatenate(weighted, axis=0)
    return matmul(weighted, kh, kl, NT)


def beside(pair):
    return jnp.where(low_lanes(32), pair[:32], pair[32:])


def kernel(
    rs, pts, basis, transfer, skel, near_list, near_count, inter_list, inter_count,
    up_t, up_s, up_list, up_count, out,
    xe, acc, f, ft, t1, t2, bb_h, bb_l, bl_h, bl_l, bu_h, bu_l,
    ce, lh, rh, ftl, eu, us, su, fu, tu, zbuf, gc, tc, qh, ql,
    in_sem, near_send, near_recv, coef_send, coef_recv, z_send, z_recv, y_send, y_recv, x_send, x_recv,
):
    g = lax.axis_index("group")
    b = lax.axis_index("bulk")
    z = lax.rem(lax.div(b, 2), 8)
    y = lax.div(b, 16)
    r = lax.rem(b, 16)
    dev = g * 64 + b

    def at(d):
        d = lax.rem(d + 256, 256)
        return (lax.div(d, 64), lax.rem(d, 64))

    right, left = at(dev + 1), at(dev - 1)

    loads = [pltpu.make_async_copy(rs, xe.at[0:32, 1024:3072], in_sem.at[0])]
    spans = (
        (128 + 32 * g + 8 * y, 8, 0),
        (64 + 16 * g + 4 * y, 4, 8),
        (32 + 8 * g + 2 * y, 2, 12),
        (16 + 4 * g, 4, 14),
        (8 + 2 * g, 2, 18),
        (4, 4, 20),
    )
    for i, (first, n, to) in enumerate(spans):
        loads.append(pltpu.make_async_copy(up_t.at[pl.ds(first, n)], eu.at[to : to + n], in_sem.at[1 + i]))
    firsts = (128 + 32 * g, 64 + 16 * g, 32 + 8 * g, 16 + 4 * g, 8 + 2 * g, 4, 2)
    for i, (first, n, to) in enumerate(zip(firsts, UPPER, UPPER_AT)):
        loads.append(pltpu.make_async_copy(up_s.at[pl.ds(first, n)], us.at[to : to + n], in_sem.at[7 + i]))
    for load in loads:
        load.start()

    barrier = pltpu.get_barrier_semaphore()

    def greet(device):
        pl.semaphore_signal(barrier, inc=1, device_id=device, device_id_type=MESH)

    greet(right)
    greet(left)

    def greet_row(k, _):
        greet((g, y * 16 + lax.rem(r + k, 16)))
        return 0

    lax.fori_loop(1, 16, greet_row, 0)
    for k in range(1, 4):
        greet((g, lax.rem(y + k, 4) * 16 + r))
        greet((lax.rem(g + k, 4), b))

    xe[32:40, 1024:3072] = jnp.zeros((8, 2048), F32)
    xe[32:35, 1024:3072] = scaled(pts[...])
    ce[32:40, :] = jnp.zeros((8, 1024), F32)
    order = ((0, 1), (2, 3), (8, 9), (12, 13), (14, 14), (10, 11), (4, 5), (6, 7))
    for i, (m, n) in enumerate(order):
        ce[32:35, i * 128 : i * 128 + 128] = scaled(jnp.concatenate([skel[m], skel[n]], axis=1))
    loads[0].wait()
    pl.semaphore_wait(barrier, 23)

    near_copies = [
        pltpu.make_async_remote_copy(
            xe.at[:, 2048:3072], xe.at[:, 0:1024], near_send.at[0], near_recv.at[0],
            device_id=right, device_id_type=MESH,
        ),
        pltpu.make_async_remote_copy(
            xe.at[:, 1024:2048], xe.at[:, 3072:4096], near_send.at[1], near_recv.at[1],
            device_id=left, device_id_type=MESH,
        ),
    ]
    for copy in near_copies:
        copy.start()

    bb_h[...], bb_l[...] = halves(basis[...])
    low128 = low_lanes(128)

    def put(to_h, to_l, at_row, value):
        n = value.shape[0]
        to_h[at_row : at_row + n, :], to_l[at_row : at_row + n, :] = halves(value)

    def twice(e):
        return jnp.concatenate([e, e], axis=1)

    for q in range(3):
        for h in range(2):
            e = twice(transfer[q * 256 + h * 128 : q * 256 + h * 128 + 128, :])
            keep = low128 if h == 0 else jnp.logical_not(low128)
            put(bl_h, bl_l, q * 256 + h * 128, jnp.where(keep, e, 0.0))
    put(bl_h, bl_l, 768, twice(transfer[768:896, :]))
    root_e = transfer[896:960, :]
    put(bl_h, bl_l, 896, twice(root_e))

    leaf = []
    for j in range(4):
        two = jnp.concatenate(
            [xe[0:32, 1024 + 512 * j : 1280 + 512 * j], xe[0:32, 1280 + 512 * j : 1536 + 512 * j]], axis=0
        )
        leaf.append(beside(matmul(two, bb_h[128 * j : 128 * j + 128, :], bb_l[128 * j : 128 * j + 128, :], NT)))

    def lift(values, h, low, first):
        joined = values[0] if len(values) == 1 else jnp.concatenate(values, axis=1)
        n = joined.shape[1]
        return matmul(joined, h[first : first + n, :], low[first : first + n, :])

    mid_a = lift(leaf[0:2], bl_h, bl_l, 0)
    mid_b = lift(leaf[2:4], bl_h, bl_l, 256)
    top = lift([mid_a, mid_b], bl_h, bl_l, 512)
    root = lift([top], bl_h, bl_l, 768)
    term = lift([root[:, 0:64]], bl_h, bl_l, 896)
    zbuf[r] = jnp.where(low_lanes(16), term[0:16], term[16:32])

    def row_copy(k, sender):
        to = lax.rem(r + k, 16)
        slot = r if sender else to
        return pltpu.make_async_remote_copy(
            zbuf.at[slot], zbuf.at[slot], z_send.at[k], z_recv.at[slot],
            device_id=(g, y * 16 + to), device_id_type=MESH,
        )

    def send_row(k, _):
        row_copy(k, True).start()
        return 0

    lax.fori_loop(1, 16, send_row, 0)
    for i, value in enumerate((leaf[0], leaf[1], mid_a, top, root, mid_b, leaf[2], leaf[3])):
        ce[0:32, i * 128 : i * 128 + 128] = value
    coef_copies = [
        pltpu.make_async_remote_copy(
            ce.at[:, 384:1024], lh, coef_send.at[0], coef_recv.at[0], device_id=right, device_id_type=MESH
        ),
        pltpu.make_async_remote_copy(
            ce.at[:, 0:640], rh, coef_send.at[1], coef_recv.at[1], device_id=left, device_id_type=MESH
        ),
    ]
    for copy in coef_copies:
        copy.start()

    near = usable(near_list[...], counted(near_count, 8, 8))
    t2[...] = mask(near, lanes(4096) // 256 + (dev * 8 - 4)) * KAPPA
    ext = lax.broadcasted_iota(jnp.int32, (16, 8), 0)
    ext_row = lax.broadcasted_iota(jnp.int32, (16, 1), 0)
    for t in range(8):
        found = jnp.where(near[t : t + 1, :] == ext + (dev * 8 - 4), 1.0, 0.0)
        column = jnp.sum(found, axis=1, keepdims=True) + jnp.where(ext_row == t + 4, 1.0, 0.0)
        t1[:, t * 256 : t * 256 + 256] = jnp.broadcast_to(column * KAPPA, (16, 256))
    t1[:, 2048:3072] = jnp.zeros((16, 1024), F32)
    acc[:, 0:2048] = NUGGET * xe[0:32, 1024:3072]
    acc[:, 2048:3072] = jnp.zeros((32, 1024), F32)
    src, tgt = features(xe[32:40, 1024:3072])
    f[:, 1024:3072] = tgt
    ft[1024:3072, :] = as_rows(src)

    def near_block(i, _):
        here = pl.multiple_of(i * 256, 256)
        x_high, x_low = halves(xe[0:32, pl.ds(here + 1024, 256)])
        x_both = jnp.concatenate([x_high, x_low], axis=0)
        m_high, m_low = halves(xe[0:32, pl.ds(here + 1280, 1024)] * t2[pl.ds(i, 1), pl.ds(here + 1280, 1024)])
        m_both = jnp.concatenate([m_high, m_low], axis=0)
        rows = ft[pl.ds(here + 1024, 256), :]
        own = jnp.zeros((32, 256), F32)
        for j in range(5):
            kh, kl = kern(dot(rows, f[:, pl.ds(here + 1024 + j * 256, 256)]))
            both = dot(x_both, kh)
            to_them = both[:32] + both[32:] + dot(x_high, kl)
            there = pl.ds(here + j * 256, 256)
            acc[:, there] += to_them * t1[pl.ds(i + 4, 1), there]
            if j > 0:
                part = slice((j - 1) * 256, j * 256)
                both = dot(m_both[:, part], kh, NT)
                own += both[:32] + both[32:] + dot(m_high[:, part], kl, NT)
        acc[:, pl.ds(here, 256)] += own
        return 0

    lax.fori_loop(0, 4, near_block, 0)

    for load in loads[1:]:
        load.wait()

    def stacked(first, n):
        return eu[first : first + n].reshape(n * 64, 64)

    for first, to in ((0, 0), (4, 256), (8, 512), (14, 896), (20, 1280)):
        for h in range(2):
            keep = low128 if h == 0 else jnp.logical_not(low128)
            put(bu_h, bu_l, to + h * 128, jnp.where(keep, twice(stacked(first + 2 * h, 2)), 0.0))
    put(bu_h, bu_l, 768, twice(stacked(12, 2)))
    put(bu_h, bu_l, 1152, twice(stacked(18, 2)))
    su[...] = jnp.zeros((8, 4352), F32)
    for i in range(34):
        su[0:3, i * 128 : i * 128 + 128] = scaled(jnp.concatenate([us[2 * i], us[2 * i + 1]], axis=1))
    fu[...] = features(su[...], "t")[0]
    places = (y * 8 + z, 32 + 4 * y + lax.div(z, 2), 48 + 2 * y + lax.div(z, 4), 56 + y, 60 + lax.div(y, 2), 62 + g, 66 + lax.div(g, 2))
    picked = jnp.concatenate(
        [jnp.concatenate([us[places[m]], us[places[n]]], axis=1) for m, n in ((0, 1), (2, 3), (4, 5), (6, 6))], axis=1
    )
    tu[...] = jnp.zeros((8, 512), F32)
    tu[0:3, :] = scaled(picked)
    ftu = as_rows(features(tu[...], "s")[0])

    def take_row(k, _):
        row_copy(k, False).wait_recv()
        return 0

    lax.fori_loop(1, 16, take_row, 0)
    low16 = low_lanes(16)
    level7 = []
    for j in range(4):
        one = zbuf[4 * j] + zbuf[4 * j + 1]
        two = zbuf[4 * j + 2] + zbuf[4 * j + 3]
        level7.append(
            jnp.concatenate(
                [jnp.where(low16, one, pltpu.roll(two, 64, 1)), jnp.where(low16, pltpu.roll(one, 64, 1), two)], axis=0
            )
        )
    level6 = [lift(level7[0:2], bu_h, bu_l, 0), lift(level7[2:4], bu_h, bu_l, 256)]
    level5 = lift(level6, bu_h, bu_l, 512)
    level4 = lift([level5], bu_h, bu_l, 768)
    for i, value in enumerate((*level7, *level6, level5, level4)):
        gc[y, :, i * 128 : i * 128 + 128] = value

    def plane_copy(k, sender):
        to = lax.rem(y + k, 4)
        slot = y if sender else to
        return pltpu.make_async_remote_copy(
            gc.at[slot], gc.at[slot], y_send.at[k], y_recv.at[slot], device_id=(g, to * 16 + r), device_id_type=MESH
        )

    for k in range(1, 4):
        plane_copy(k, True).start()

    for copy in near_copies:
        copy.wait_recv()
    src, tgt = features(xe[32:40, 0:1024])
    ft[0:1024, :] = as_rows(src)
    src, tgt = features(xe[32:40, 3072:4096])
    f[:, 3072:4096] = tgt
    lax.fori_loop(4, 8, near_block, 0)

    for k in range(1, 4):
        plane_copy(k, False).wait_recv()
    low32 = low_lanes(32)
    level4 = [
        jnp.where(low32, gc[0, :, 896:1024], gc[1, :, 896:1024]),
        jnp.where(low32, gc[2, :, 896:1024], gc[3, :, 896:1024]),
    ]
    level3 = lift(level4, bu_h, bu_l, 896)
    tc[g] = lift([level3], bu_h, bu_l, 1152)

    def group_copy(k, sender):
        to = lax.rem(g + k, 4)
        slot = g if sender else to
        return pltpu.make_async_remote_copy(
            tc.at[slot], tc.at[slot], x_send.at[k], x_recv.at[slot], device_id=(to, b), device_id_type=MESH
        )

    for k in range(1, 4):
        group_copy(k, True).start()

    for e in range(4):
        x_high, x_low = halves(xe[0:32, e * 256 : e * 256 + 256])
        x_both = jnp.concatenate([x_high, x_low], axis=0)
        for t in range(e + 1):
            kh, kl = kern(dot(ft[e * 256 : e * 256 + 256, :], f[:, 1024 + t * 256 : 1280 + t * 256]))
            both = dot(x_both, kh)
            there = slice(t * 256, t * 256 + 256)
            acc[:, there] += (both[:32] + both[32:] + dot(x_high, kl)) * t1[e : e + 1, there]

    for copy in coef_copies:
        copy.wait_recv()
    ftl[...] = as_rows(features(ce[32:40, :], "s")[0])
    inter = usable(inter_list[...], counted(inter_count, 15, 8))
    table = jnp.concatenate([lh[:, 384:640], ce[:, 0:256], ce[:, 768:1024], rh[:, 0:256]], axis=1)
    feats = features(table[32:40], "t")[0]
    found = mask(inter[0:8], lanes(1024) // 64 + (dev * 8 - 4))
    field0 = []
    for j, at_lane in enumerate((0, 128, 768, 896)):
        part = slice(j * 128, j * 128 + 640)
        masks = [found[2 * j : 2 * j + 1, part], found[2 * j + 1 : 2 * j + 2, part]]
        field0.append(beside(couple(ftl[at_lane : at_lane + 128, :], feats[:, part], table[0:32, part], masks)))
    table = jnp.concatenate([lh[:, 256:384], ce[:, 256:384], ce[:, 640:768], rh[:, 256:384]], axis=1)
    feats = features(table[32:40], "t")[0]
    found = mask(inter[8:12], lanes(512) // 64 + (dev * 4 - 2))
    field1 = []
    for j, at_lane in enumerate((256, 640)):
        part = slice(j * 128, j * 128 + 384)
        masks = [found[2 * j : 2 * j + 1, part], found[2 * j + 1 : 2 * j + 2, part]]
        field1.append(beside(couple(ftl[at_lane : at_lane + 128, :], feats[:, part], table[0:32, part], masks)))
    table = jnp.concatenate([lh[:, 0:128], ce[:, 384:512], rh[:, 384:512]], axis=1)
    feats = features(table[32:40], "t")[0]
    found = mask(inter[12:14], lanes(384) // 64 + (dev * 2 - 2))
    field2 = beside(couple(ftl[384:512, :], feats, table[0:32], [found[0:1], found[1:2]]))
    table = jnp.concatenate([lh[:, 128:256], ce[:, 512:640], rh[:, 512:640]], axis=1)
    feats = features(table[32:40], "t")[0]
    spot = lanes(384)
    ids = jnp.where(lax.rem(spot, 128) < 64, spot // 128 + (dev - 1), -1)
    found = mask(inter[14:15], ids)
    field3 = beside(couple(ftl[512:640, :], feats, table[0:32], [found, found]))

    path = (z, 8 + lax.div(z, 2), 12 + lax.div(z, 4), 14 + y, 18 + lax.div(y, 2), 20 + g)
    product = jnp.concatenate([root_e, root_e], axis=0)
    for i in range(7):
        if i > 0:
            product = matmul(product, *halves(eu[path[i - 1]]))
        qh[i], ql[i] = halves(product)

    def path_field(i, coefs):
        h = firsts[i] + places[i] - UPPER_AT[i]
        first, n = UPPER_AT[i] * 64, UPPER[i] * 64
        listed = usable(up_list[pl.ds(h, 1), :], up_count[h])
        found = mask(listed, lanes(n) // 64 + firsts[i])
        field = couple(ftu[i * 64 : i * 64 + 64, :], fu[:, first : first + n], coefs, [found])
        return matmul(field, qh[i], ql[i], NT)

    incoming = path_field(0, jnp.concatenate([gc[k, :, 0:512] for k in range(4)], axis=1))
    incoming += path_field(1, jnp.concatenate([gc[k, :, 512:768] for k in range(4)], axis=1))
    incoming += path_field(2, jnp.concatenate([gc[k, :, 768:896] for k in range(4)], axis=1))
    incoming += path_field(3, jnp.concatenate(level4, axis=1))
    incoming += path_field(4, level3)
    for k in range(1, 4):
        group_copy(k, False).wait_recv()
    level2 = [jnp.where(low32, tc[0], tc[1]), jnp.where(low32, tc[2], tc[3])]
    incoming += path_field(5, jnp.concatenate(level2, axis=1))
    incoming += path_field(6, lift(level2, bu_h, bu_l, 1280))

    def lower(value, first, n):
        return matmul(value, bl_h[first : first + n, :], bl_l[first : first + n, :], NT)

    down3 = jnp.where(low32, field3 + incoming, 0.0)
    down2 = field2 + lower(down3, 768, 128)
    down1 = lower(down2, 512, 256)
    down1 = [field1[0] + down1[:, 0:128], field1[1] + down1[:, 128:256]]
    for q in range(2):
        down0 = lower(down1[q], q * 256, 256)
        for h in range(2):
            j = 2 * q + h
            pair = field0[j] + down0[:, h * 128 : h * 128 + 128]
            two = jnp.concatenate([jnp.where(low32, pair, 0.0), jnp.where(low32, 0.0, pair)], axis=0)
            far = matmul(two, bb_h[128 * j : 128 * j + 128, :], bb_l[128 * j : 128 * j + 128, :])
            for k in range(2):
                part = slice((2 * j + k) * 256, (2 * j + k) * 256 + 256)
                out[:, part] = acc[:, part] + far[32 * k : 32 * k + 32]

    for copy in near_copies + coef_copies:
        copy.wait_send()

    def sent_row(k, _):
        row_copy(k, True).wait_send()
        return 0

    lax.fori_loop(1, 16, sent_row, 0)
    for k in range(1, 4):
        plane_copy(k, True).wait_send()
        group_copy(k, True).wait_send()


def on_device(
    rs, pts, basis, transfer, skel, near_list, near_count, inter_list, inter_count, up_t, up_s, up_list, up_count
):
    vmem = pl.BlockSpec(memory_space=pltpu.VMEM)
    smem = pl.BlockSpec(memory_space=pltpu.SMEM)
    anywhere = pl.BlockSpec(memory_space=pl.ANY)
    dma = pltpu.SemaphoreType.DMA
    return pl.pallas_call(
        kernel,
        out_shape=jax.ShapeDtypeStruct((32, 2048), F32),
        in_specs=[anywhere, vmem, vmem, vmem, vmem, vmem, smem, vmem, smem, anywhere, anywhere, vmem, smem],
        out_specs=vmem,
        scratch_shapes=[
            pltpu.VMEM((40, 4096), F32),
            pltpu.VMEM((32, 3072), F32),
            pltpu.VMEM((FEATS, 4096), BF16),
            pltpu.VMEM((3072, FEATS), BF16),
            pltpu.VMEM((16, 3072), F32),
            pltpu.VMEM((8, 4096), F32),
            pltpu.VMEM((512, 256), BF16),
            pltpu.VMEM((512, 256), BF16),
            pltpu.VMEM((960, 128), BF16),
            pltpu.VMEM((960, 128), BF16),
            pltpu.VMEM((1536, 128), BF16),
            pltpu.VMEM((1536, 128), BF16),
            pltpu.VMEM((40, 1024), F32),
            pltpu.VMEM((40, 640), F32),
            pltpu.VMEM((40, 640), F32),
            pltpu.VMEM((1024, FEATS), BF16),
            pltpu.VMEM((24, 64, 64), F32),
            pltpu.VMEM((68, 3, 64), F32),
            pltpu.VMEM((8, 4352), F32),
            pltpu.VMEM((FEATS, 4352), BF16),
            pltpu.VMEM((8, 512), F32),
            pltpu.VMEM((16, 16, 128), F32),
            pltpu.VMEM((4, 32, 1024), F32),
            pltpu.VMEM((4, 32, 128), F32),
            pltpu.VMEM((7, 128, 64), BF16),
            pltpu.VMEM((7, 128, 64), BF16),
            dma((14,)),
            dma((2,)), dma((2,)), dma((2,)), dma((2,)),
            dma((16,)), dma((16,)), dma((4,)), dma((4,)), dma((4,)), dma((4,)),
        ],
        compiler_params=pltpu.CompilerParams(
            collective_id=0, has_side_effects=True, vmem_limit_bytes=48 * 2**20
        ),
    )(
        rs, pts, basis.reshape(512, 256), transfer.reshape(960, 64), skel, near_list, near_count, inter_list,
        inter_count, up_t, up_s, up_list, up_count,
    )


def solution(mesh):
    both = ("group", "bulk")
    in_specs = (
        P(None, both),
        P(None, both),
        P(both, None, None),
        P(both, None, None),
        P(both, None, None),
        P(both, None),
        P(both),
        P(both, None),
        P(both),
        P(),
        P(),
        P(),
        P(),
    )
    return jax.shard_map(
        on_device, mesh=mesh, in_specs=in_specs, out_specs=P(None, both), check_vma=False
    )
```

profile of v0, /device:TPU:2, one launch (start us, length us, event | category | flops | bytes accessed | tf_op | source)
XLA Modules:
  0.0 47.7 jit_solution(1386608878917812948)
XLA Ops:
  0.0 0.0 copy-start.5
  0.0 0.0 copy-start.7
  0.0 0.0 copy-start.6
  0.0 0.0 copy-start.4
  0.0 0.0 copy-start.1
  0.0 0.0 copy-start
  0.0 0.0 copy-start.3
  0.0 0.0 copy-start.2
  0.1 0.9 %copy.15.inter_list = s32[15,8]{1,0:T(8,128)S(1)} copy(s32[15,8]{0,1:T(8,128)} %param.20) | data formatting | bytes 960 | tf_op args[7]
  0.9 0.8 %copy.14.skel = f32[15,3,64]{2,1,0:T(4,128)S(1)} copy(f32[15,3,64]{2,0,1:T(8,128)} %param.17) | data formatting | bytes 23040 | tf_op args[4]
  1.7 0.8 %copy.18.up_list = s32[256,8]{1,0:T(8,128)S(1)} copy(s32[256,8]{0,1:T(8,128)} %param.24) | data formatting | bytes 16384 | tf_op args[11]
  2.5 1.2 %copy.17.up_s = f32[256,3,64]{2,1,0:T(4,128)S(1)} copy(f32[256,3,64]{0,2,1:T(8,128)} %param.23) | data formatting | bytes 393216 | tf_op args[10]
  3.7 9.2 %copy.16.up_t = f32[256,64,64]{2,1,0:T(8,128)} copy(f32[256,64,64]{0,2,1:T(8,128)} %param.22) | data formatting | bytes 8388608 | tf_op args[9]
  12.8 0.0 copy-done.5
  12.8 0.0 copy-done.7
  12.8 0.0 copy-done.6
  12.8 0.0 copy-done.4
  12.9 0.0 copy-done.1
  12.9 0.0 copy-done
  12.9 0.0 copy-done.3
  12.9 0.0 copy-done.2
  12.9 34.1 %shard_map.127 = f32[32,2048]{1,0:T(8,128)S(1)} custom-call(f32[32,2048]{1,0:T(8,128)S(1)} %copy-done.2, f32[3,2048]{1,0:T(4,128)S(1)} %copy-done.3, f32[512,256]{1,0:T(8,128)S(1)} %bitcast.2, f32[960,64]{1,0:T(8,128)S(1)} %bitcast.3, f32[15,3,64]{2,1,0:T(4,128)S(1)} %copy.14.skel, s32[8,8]{1,0:T(8,128)S(1)} %copy-done.4, s32[8]{0:T(128)S(1)} %copy-done.6, ...), custom_call_target="tpu_custom_call" | custom-call | tf_op jit(solution)/shard_map/pallas_call | solution.py:483
  47.0 0.7 %copy.20 = f32[32,2048]{1,0:T(8,128)} copy(f32[32,2048]{1,0:T(8,128)S(1)} %shard_map.127) | data formatting | bytes 524288
Async XLA Ops:
  0.0 12.8 %copy-start.5 = (s32[256]{0:T(256)S(1)}, s32[256]{0:T(256)}, u32[]{:S(2)}) copy-start(s32[256]{0:T(256)} %up_count.1) | copy-start | bytes 3076
  0.0 12.8 %copy-start.7 = (s32[15]{0:T(128)S(1)}, s32[15]{0:T(128)}, u32[]{:S(2)}) copy-start(s32[15]{0:T(128)} %inter_count.1) | copy-start | bytes 184
  0.0 12.8 %copy-start.6 = (s32[8]{0:T(128)S(1)}, s32[8]{0:T(128)}, u32[]{:S(2)}) copy-start(s32[8]{0:T(128)} %near_count.1) | copy-start | bytes 100
  0.0 12.8 %copy-start.4 = (s32[8,8]{1,0:T(8,128)S(1)}, s32[8,8]{1,0:T(8,128)}, u32[]{:S(2)}) copy-start(s32[8,8]{1,0:T(8,128)} %near_list.1) | copy-start | bytes 772
  0.0 12.8 %copy-start.1 = (f32[15,64,64]{2,1,0:T(8,128)S(1)}, f32[15,64,64]{2,1,0:T(8,128)}, u32[]{:S(2)}) copy-start(f32[15,64,64]{2,1,0:T(8,128)} %param.16) | copy-start | bytes 737284
  0.0 12.8 %copy-start = (f32[8,64,256]{2,1,0:T(8,128)S(1)}, f32[8,64,256]{2,1,0:T(8,128)}, u32[]{:S(2)}) copy-start(f32[8,64,256]{2,1,0:T(8,128)} %param.15) | copy-start | bytes 1572868
  0.0 12.8 %copy-start.3 = (f32[3,2048]{1,0:T(4,128)S(1)}, f32[3,2048]{1,0:T(4,128)}, u32[]{:S(2)}) copy-start(f32[3,2048]{1,0:T(4,128)} %pts.1) | copy-start | bytes 73732
  0.0 12.8 %copy-start.2 = (f32[32,2048]{1,0:T(8,128)S(1)}, f32[32,2048]{1,0:T(8,128)}, u32[]{:S(2)}) copy-start(f32[32,2048]{1,0:T(8,128)} %rs.1) | copy-start | bytes 786436
where the time goes:
time: 48.6 us; the launch traced here: 47.7 us
  Pallas kernels  34.1 us (70%)
  local copies, waits for them, and re-layouts  13.5 us (28%)
    pallas_call x1, Pallas kernels, on_device(): pl.pallas_call(kernel, out_shape=jax.ShapeDtypeStruct((32, 2048), F32), i...  34.1 us
    unnamed x22, local copies, waits for them, and re-layouts  13.5 us

commit v1 on v0

--- a/solution.py
+++ b/solution.py
@@ -22,7 +22,6 @@
 NUGGET = 0.5
 FEATS = 48
 UPPER = (32, 16, 8, 4, 2, 4, 2)
-UPPER_AT = (0, 32, 48, 56, 60, 62, 66)
 
 
 def dot(a, b, dims=NN):
@@ -116,10 +115,11 @@
 
 
 def kernel(
-    rs, pts, basis, transfer, skel, near_list, near_count, inter_list, inter_count,
-    up_t, up_s, up_list, up_count, out,
-    xe, acc, f, ft, t1, t2, bb_h, bb_l, bl_h, bl_l, bu_h, bu_l,
-    ce, lh, rh, ftl, eu, us, su, fu, tu, zbuf, gc, tc, qh, ql,
+    rs, pts_in, basis_in, transfer_in, skel_in, near_list_in, near_count_in, inter_list_in, inter_count_in,
+    up_t, up_s, up_list_in, up_count_in, out,
+    xe, acc, f, ft, t2, bb_h, bb_l, bl_h, bl_l, bu_h, bu_l,
+    ce, lh, rh, ftl, ev, et, sv, st, su, fu, tu, zbuf, gc, tc, qh, ql,
+    pts, basis, transfer, skel, near_list, near_count, inter_list, inter_count, up_list, up_count,
     in_sem, near_send, near_recv, coef_send, coef_recv, z_send, z_recv, y_send, y_recv, x_send, x_recv,
 ):
     g = lax.axis_index("group")
@@ -135,22 +135,26 @@
 
     right, left = at(dev + 1), at(dev - 1)
 
-    loads = [pltpu.make_async_copy(rs, xe.at[0:32, 1024:3072], in_sem.at[0])]
-    spans = (
-        (128 + 32 * g + 8 * y, 8, 0),
-        (64 + 16 * g + 4 * y, 4, 8),
-        (32 + 8 * g + 2 * y, 2, 12),
-        (16 + 4 * g, 4, 14),
-        (8 + 2 * g, 2, 18),
-        (4, 4, 20),
+    pairs = (
+        (rs, xe.at[0:32, 1024:3072]),
+        (pts_in, pts),
+        (skel_in, skel),
+        (basis_in, basis),
+        (transfer_in, transfer),
+        (near_list_in, near_list),
+        (near_count_in, near_count),
+        (inter_list_in, inter_list),
+        (inter_count_in, inter_count),
+        (up_list_in, up_list),
+        (up_count_in, up_count),
+        (up_s, sv),
+        (up_t.at[:, 128:256], ev.at[0:4096]),
+        (up_t.at[:, 0:128], ev.at[4096:8192]),
     )
-    for i, (first, n, to) in enumerate(spans):
-        loads.append(pltpu.make_async_copy(up_t.at[pl.ds(first, n)], eu.at[to : to + n], in_sem.at[1 + i]))
-    firsts = (128 + 32 * g, 64 + 16 * g, 32 + 8 * g, 16 + 4 * g, 8 + 2 * g, 4, 2)
-    for i, (first, n, to) in enumerate(zip(firsts, UPPER, UPPER_AT)):
-        loads.append(pltpu.make_async_copy(up_s.at[pl.ds(first, n)], us.at[to : to + n], in_sem.at[7 + i]))
+    loads = [pltpu.make_async_copy(of, to, in_sem.at[i]) for i, (of, to) in enumerate(pairs)]
     for load in loads:
         load.start()
+    firsts = (128 + 32 * g, 64 + 16 * g, 32 + 8 * g, 16 + 4 * g, 8 + 2 * g, 4, 2)
 
     barrier = pltpu.get_barrier_semaphore()
 
@@ -170,11 +174,13 @@
         greet((lax.rem(g + k, 4), b))
 
     xe[32:40, 1024:3072] = jnp.zeros((8, 2048), F32)
+    loads[1].wait()
+    loads[2].wait()
     xe[32:35, 1024:3072] = scaled(pts[...])
     ce[32:40, :] = jnp.zeros((8, 1024), F32)
     order = ((0, 1), (2, 3), (8, 9), (12, 13), (14, 14), (10, 11), (4, 5), (6, 7))
     for i, (m, n) in enumerate(order):
-        ce[32:35, i * 128 : i * 128 + 128] = scaled(jnp.concatenate([skel[m], skel[n]], axis=1))
+        ce[32:35, i * 128 : i * 128 + 128] = scaled(jnp.concatenate([skel[:, m, :], skel[:, n, :]], axis=1))
     loads[0].wait()
     pl.semaphore_wait(barrier, 23)
 
@@ -191,6 +197,8 @@
     for copy in near_copies:
         copy.start()
 
+    loads[3].wait()
+    loads[4].wait()
     bb_h[...], bb_l[...] = halves(basis[...])
     low128 = low_lanes(128)
 
@@ -255,67 +263,96 @@
     for copy in coef_copies:
         copy.start()
 
+    for load in loads[5:11]:
+        load.wait()
     near = usable(near_list[...], counted(near_count, 8, 8))
-    t2[...] = mask(near, lanes(4096) // 256 + (dev * 8 - 4)) * KAPPA
-    ext = lax.broadcasted_iota(jnp.int32, (16, 8), 0)
-    ext_row = lax.broadcasted_iota(jnp.int32, (16, 1), 0)
-    for t in range(8):
-        found = jnp.where(near[t : t + 1, :] == ext + (dev * 8 - 4), 1.0, 0.0)
-        column = jnp.sum(found, axis=1, keepdims=True) + jnp.where(ext_row == t + 4, 1.0, 0.0)
-        t1[:, t * 256 : t * 256 + 256] = jnp.broadcast_to(column * KAPPA, (16, 256))
-    t1[:, 2048:3072] = jnp.zeros((16, 1024), F32)
-    acc[:, 0:2048] = NUGGET * xe[0:32, 1024:3072]
-    acc[:, 2048:3072] = jnp.zeros((32, 1024), F32)
+    ids = lanes(4096) // 256
+    itself = lax.broadcasted_iota(jnp.int32, (8, 1), 0) + 4 == ids
+    t2[...] = (mask(near, ids + (dev * 8 - 4)) + jnp.where(itself, 1.0, 0.0)) * KAPPA
     src, tgt = features(xe[32:40, 1024:3072])
-    f[:, 1024:3072] = tgt
+    f[...] = tgt
     ft[1024:3072, :] = as_rows(src)
 
-    def near_block(i, _):
-        here = pl.multiple_of(i * 256, 256)
-        x_high, x_low = halves(xe[0:32, pl.ds(here + 1024, 256)])
-        x_both = jnp.concatenate([x_high, x_low], axis=0)
-        m_high, m_low = halves(xe[0:32, pl.ds(here + 1280, 1024)] * t2[pl.ds(i, 1), pl.ds(here + 1280, 1024)])
-        m_both = jnp.concatenate([m_high, m_low], axis=0)
-        rows = ft[pl.ds(here + 1024, 256), :]
-        own = jnp.zeros((32, 256), F32)
-        for j in range(5):
-            kh, kl = kern(dot(rows, f[:, pl.ds(here + 1024 + j * 256, 256)]))
-            both = dot(x_both, kh)
-            to_them = both[:32] + both[32:] + dot(x_high, kl)
-            there = pl.ds(here + j * 256, 256)
-            acc[:, there] += to_them * t1[pl.ds(i + 4, 1), there]
-            if j > 0:
-                part = slice((j - 1) * 256, j * 256)
-                both = dot(m_both[:, part], kh, NT)
-                own += both[:32] + both[32:] + dot(m_high[:, part], kl, NT)
-        acc[:, pl.ds(here, 256)] += own
-        return 0
-
-    lax.fori_loop(0, 4, near_block, 0)
-
-    for load in loads[1:]:
+    def near_leaf(t, first, last):
+        targets = f[:, t * 256 : t * 256 + 256]
+        total = jnp.zeros((32, 256), F32)
+        for e in range(first, last):
+            part = slice(e * 256, e * 256 + 256)
+            x_high, x_low = halves(xe[0:32, part] * t2[t : t + 1, part])
+            kh, kl = kern(dot(ft[part, :], targets))
+            both = dot(jnp.concatenate([x_high, x_low], axis=0), kh)
+            total += both[:32] + both[32:] + dot(x_high, kl)
+        return total
+
+    def own_leaf(t):
+        part = slice(t * 256, t * 256 + 256)
+        nugget = NUGGET * xe[0:32, t * 256 + 1024 : t * 256 + 1280]
+        acc[:, part] = nugget + near_leaf(t, max(t, 4), min(t + 9, 12))
+
+    with jax.named_scope("near_a"):
+        for t in range(4):
+            own_leaf(t)
+
+    for load in loads[11:14]:
         load.wait()
 
-    def stacked(first, n):
-        return eu[first : first + n].reshape(n * 64, 64)
-
-    for first, to in ((0, 0), (4, 256), (8, 512), (14, 896), (20, 1280)):
-        for h in range(2):
-            keep = low128 if h == 0 else jnp.logical_not(low128)
-            put(bu_h, bu_l, to + h * 128, jnp.where(keep, twice(stacked(first + 2 * h, 2)), 0.0))
-    put(bu_h, bu_l, 768, twice(stacked(12, 2)))
-    put(bu_h, bu_l, 1152, twice(stacked(18, 2)))
-    su[...] = jnp.zeros((8, 4352), F32)
-    for i in range(34):
-        su[0:3, i * 128 : i * 128 + 128] = scaled(jnp.concatenate([us[2 * i], us[2 * i + 1]], axis=1))
-    fu[...] = features(su[...], "t")[0]
-    places = (y * 8 + z, 32 + 4 * y + lax.div(z, 2), 48 + 2 * y + lax.div(z, 4), 56 + y, 60 + lax.div(y, 2), 62 + g, 66 + lax.div(g, 2))
-    picked = jnp.concatenate(
-        [jnp.concatenate([us[places[m]], us[places[n]]], axis=1) for m, n in ((0, 1), (2, 3), (4, 5), (6, 6))], axis=1
-    )
-    tu[...] = jnp.zeros((8, 512), F32)
-    tu[0:3, :] = scaled(picked)
-    ftu = as_rows(features(tu[...], "s")[0])
+    with jax.named_scope("upper_weights"):
+        def turn(i, _):
+            half, k = lax.div(i, 32), lax.rem(i, 32)
+            first = pl.multiple_of(half * 4096 + k * 64, 64)
+            block = jnp.concatenate([ev[pl.ds(first, 64), :], ev[pl.ds(first + 2048, 64), :]], axis=0)
+            et[pl.ds(pl.multiple_of(i * 128, 128), 128), :] = block.T
+            return 0
+
+        lax.fori_loop(0, 64, turn, 0, unroll=4)
+
+        def edge(h, half):
+            two = et[pl.ds(half * 4096 + h - (128 if half == 0 else 0), 32, stride=128), :]
+            other = pltpu.roll(two, 64, 1)
+            low = low_lanes(32)
+            return jnp.concatenate([jnp.where(low, two, other), jnp.where(low, other, two)], axis=0)
+
+        nodes = (
+            (128 + 32 * g + 8 * y, 0, 0),
+            (132 + 32 * g + 8 * y, 0, 256),
+            (64 + 16 * g + 4 * y, 1, 512),
+            (16 + 4 * g, 1, 896),
+            (4, 1, 1280),
+        )
+        low64 = low_lanes(64)
+        for first, half, to in nodes:
+            for n in range(4):
+                keep = low64 if n < 2 else jnp.logical_not(low64)
+                put(bu_h, bu_l, to + n * 64, jnp.where(keep, edge(first + n, half), 0.0))
+        for first, to in ((32 + 8 * g + 2 * y, 768), (8 + 2 * g, 1152)):
+            for n in range(2):
+                put(bu_h, bu_l, to + n * 64, edge(first + n, 1))
+    with jax.named_scope("upper_skeletons"):
+        su[...] = jnp.zeros((8, 4352), F32)
+        for c in range(3):
+            for h in range(2):
+                first = h * 128
+                block = jnp.concatenate([sv[c * 64 : c * 64 + 64, first : first + 128]] * 2, axis=0)
+                st[c, first : first + 128, :] = block.T
+        at_lane = 0
+        for first, n in zip(firsts, UPPER):
+            for i in range(n // 2):
+                one, two = st[:, pl.ds(first + 2 * i, 1), :], st[:, pl.ds(first + 2 * i + 1, 1), :]
+                pair = jnp.where(lax.broadcasted_iota(jnp.int32, (3, 1, 128), 2) < 64, one, two)
+                su[0:3, at_lane : at_lane + 128] = scaled(pair.reshape(3, 128))
+                at_lane += 128
+        fu[...] = features(su[...], "t")[0]
+        heap = [lax.div(256 + dev, 2 ** (i + 1)) for i in range(7)]
+        tu[...] = jnp.zeros((8, 512), F32)
+        for i, (m, n) in enumerate(((0, 1), (2, 3), (4, 5), (6, 6))):
+            one, two = st[:, pl.ds(heap[m], 1), :], st[:, pl.ds(heap[n], 1), :]
+            pair = jnp.where(lax.broadcasted_iota(jnp.int32, (3, 1, 128), 2) < 64, one, two)
+            tu[0:3, i * 128 : i * 128 + 128] = scaled(pair.reshape(3, 128))
+        ftu = as_rows(features(tu[...], "s")[0])
+
+    with jax.named_scope("near_b"):
+        for t in range(4, 8):
+            own_leaf(t)
 
     def take_row(k, _):
         row_copy(k, False).wait_recv()
@@ -350,11 +387,13 @@
 
     for copy in near_copies:
         copy.wait_recv()
-    src, tgt = features(xe[32:40, 0:1024])
-    ft[0:1024, :] = as_rows(src)
-    src, tgt = features(xe[32:40, 3072:4096])
-    f[:, 3072:4096] = tgt
-    lax.fori_loop(4, 8, near_block, 0)
+    with jax.named_scope("near_c"):
+        src = features(xe[32:40, 0:1024], "s")[0]
+        ft[0:1024, :] = as_rows(src)
+        src = features(xe[32:40, 3072:4096], "s")[0]
+        ft[3072:4096, :] = as_rows(src)
+        for t in range(4):
+            acc[:, t * 256 : t * 256 + 256] += near_leaf(t, t, 4)
 
     for k in range(1, 4):
         plane_copy(k, False).wait_recv()
@@ -376,58 +415,66 @@
     for k in range(1, 4):
         group_copy(k, True).start()
 
-    for e in range(4):
-        x_high, x_low = halves(xe[0:32, e * 256 : e * 256 + 256])
-        x_both = jnp.concatenate([x_high, x_low], axis=0)
-        for t in range(e + 1):
-            kh, kl = kern(dot(ft[e * 256 : e * 256 + 256, :], f[:, 1024 + t * 256 : 1280 + t * 256]))
-            both = dot(x_both, kh)
-            there = slice(t * 256, t * 256 + 256)
-            acc[:, there] += (both[:32] + both[32:] + dot(x_high, kl)) * t1[e : e + 1, there]
+    with jax.named_scope("near_d"):
+        for t in range(4, 8):
+            acc[:, t * 256 : t * 256 + 256] += near_leaf(t, 12, t + 9)
 
     for copy in coef_copies:
         copy.wait_recv()
     ftl[...] = as_rows(features(ce[32:40, :], "s")[0])
-    inter = usable(inter_list[...], counted(inter_count, 15, 8))
+    spot = lax.broadcasted_iota(jnp.int32, (8, 15), 1)
+    slot = lax.broadcasted_iota(jnp.int32, (8, 15), 0)
+    counts = jnp.zeros((8, 15), jnp.int32)
+    for n in range(15):
+        counts = jnp.where(spot == n, inter_count[n], counts)
+    inter = jnp.where(slot < counts, inter_list[...], -1000)
+
+    def listed(n, ids):
+        return jnp.sum(jnp.where(inter[:, n : n + 1] == ids, 1.0, 0.0), axis=0, keepdims=True)
+
     table = jnp.concatenate([lh[:, 384:640], ce[:, 0:256], ce[:, 768:1024], rh[:, 0:256]], axis=1)
     feats = features(table[32:40], "t")[0]
-    found = mask(inter[0:8], lanes(1024) // 64 + (dev * 8 - 4))
+    ids = lanes(1024) // 64 + (dev * 8 - 4)
     field0 = []
     for j, at_lane in enumerate((0, 128, 768, 896)):
         part = slice(j * 128, j * 128 + 640)
-        masks = [found[2 * j : 2 * j + 1, part], found[2 * j + 1 : 2 * j + 2, part]]
+        masks = [listed(2 * j, ids[:, part]), listed(2 * j + 1, ids[:, part])]
         field0.append(beside(couple(ftl[at_lane : at_lane + 128, :], feats[:, part], table[0:32, part], masks)))
     table = jnp.concatenate([lh[:, 256:384], ce[:, 256:384], ce[:, 640:768], rh[:, 256:384]], axis=1)
     feats = features(table[32:40], "t")[0]
-    found = mask(inter[8:12], lanes(512) // 64 + (dev * 4 - 2))
+    ids = lanes(512) // 64 + (dev * 4 - 2)
     field1 = []
     for j, at_lane in enumerate((256, 640)):
         part = slice(j * 128, j * 128 + 384)
-        masks = [found[2 * j : 2 * j + 1, part], found[2 * j + 1 : 2 * j + 2, part]]
+        masks = [listed(8 + 2 * j, ids[:, part]), listed(9 + 2 * j, ids[:, part])]
         field1.append(beside(couple(ftl[at_lane : at_lane + 128, :], feats[:, part], table[0:32, part], masks)))
     table = jnp.concatenate([lh[:, 0:128], ce[:, 384:512], rh[:, 384:512]], axis=1)
     feats = features(table[32:40], "t")[0]
-    found = mask(inter[12:14], lanes(384) // 64 + (dev * 2 - 2))
-    field2 = beside(couple(ftl[384:512, :], feats, table[0:32], [found[0:1], found[1:2]]))
+    ids = lanes(384) // 64 + (dev * 2 - 2)
+    field2 = beside(couple(ftl[384:512, :], feats, table[0:32], [listed(12, ids), listed(13, ids)]))
     table = jnp.concatenate([lh[:, 128:256], ce[:, 512:640], rh[:, 512:640]], axis=1)
     feats = features(table[32:40], "t")[0]
     spot = lanes(384)
     ids = jnp.where(lax.rem(spot, 128) < 64, spot // 128 + (dev - 1), -1)
-    found = mask(inter[14:15], ids)
+    found = listed(14, ids)
     field3 = beside(couple(ftl[512:640, :], feats, table[0:32], [found, found]))
 
-    path = (z, 8 + lax.div(z, 2), 12 + lax.div(z, 4), 14 + y, 18 + lax.div(y, 2), 20 + g)
     product = jnp.concatenate([root_e, root_e], axis=0)
     for i in range(7):
         if i > 0:
-            product = matmul(product, *halves(eu[path[i - 1]]))
+            product = matmul(product, *halves(edge(heap[i - 1], 0 if i == 1 else 1)[:, 0:64]))
         qh[i], ql[i] = halves(product)
+    node = lax.broadcasted_iota(jnp.int32, (8, 256), 1)
+    up_slots = lax.broadcasted_iota(jnp.int32, (8, 1), 0)
+    up_lists = up_list[...].astype(F32)
 
     def path_field(i, coefs):
-        h = firsts[i] + places[i] - UPPER_AT[i]
-        first, n = UPPER_AT[i] * 64, UPPER[i] * 64
-        listed = usable(up_list[pl.ds(h, 1), :], up_count[h])
-        found = mask(listed, lanes(n) // 64 + firsts[i])
+        h = heap[i]
+        first, n = sum(UPPER[:i]) * 64, UPPER[i] * 64
+        column = jnp.sum(jnp.where(node == h, up_lists, 0.0), axis=1, keepdims=True)
+        column = jnp.where(up_slots < up_count[h], column, -1000.0)
+        ids = (lanes(n) // 64 + firsts[i]).astype(F32)
+        found = jnp.sum(jnp.where(column == ids, 1.0, 0.0), axis=0, keepdims=True)
         field = couple(ftu[i * 64 : i * 64 + 64, :], fu[:, first : first + n], coefs, [found])
         return matmul(field, qh[i], ql[i], NT)
 
@@ -477,20 +524,18 @@
     rs, pts, basis, transfer, skel, near_list, near_count, inter_list, inter_count, up_t, up_s, up_list, up_count
 ):
     vmem = pl.BlockSpec(memory_space=pltpu.VMEM)
-    smem = pl.BlockSpec(memory_space=pltpu.SMEM)
     anywhere = pl.BlockSpec(memory_space=pl.ANY)
     dma = pltpu.SemaphoreType.DMA
     return pl.pallas_call(
         kernel,
         out_shape=jax.ShapeDtypeStruct((32, 2048), F32),
-        in_specs=[anywhere, vmem, vmem, vmem, vmem, vmem, smem, vmem, smem, anywhere, anywhere, vmem, smem],
+        in_specs=[anywhere] * 13,
         out_specs=vmem,
         scratch_shapes=[
             pltpu.VMEM((40, 4096), F32),
-            pltpu.VMEM((32, 3072), F32),
-            pltpu.VMEM((FEATS, 4096), BF16),
-            pltpu.VMEM((3072, FEATS), BF16),
-            pltpu.VMEM((16, 3072), F32),
+            pltpu.VMEM((32, 2048), F32),
+            pltpu.VMEM((FEATS, 2048), BF16),
+            pltpu.VMEM((4096, FEATS), BF16),
             pltpu.VMEM((8, 4096), F32),
             pltpu.VMEM((512, 256), BF16),
             pltpu.VMEM((512, 256), BF16),
@@ -502,8 +547,10 @@
             pltpu.VMEM((40, 640), F32),
             pltpu.VMEM((40, 640), F32),
             pltpu.VMEM((1024, FEATS), BF16),
-            pltpu.VMEM((24, 64, 64), F32),
-            pltpu.VMEM((68, 3, 64), F32),
+            pltpu.VMEM((8192, 128), F32),
+            pltpu.VMEM((8192, 128), F32),
+            pltpu.VMEM((192, 256), F32),
+            pltpu.VMEM((3, 256, 128), F32),
             pltpu.VMEM((8, 4352), F32),
             pltpu.VMEM((FEATS, 4352), BF16),
             pltpu.VMEM((8, 512), F32),
@@ -512,16 +559,27 @@
             pltpu.VMEM((4, 32, 128), F32),
             pltpu.VMEM((7, 128, 64), BF16),
             pltpu.VMEM((7, 128, 64), BF16),
+            pltpu.VMEM((3, 2048), F32),
+            pltpu.VMEM((512, 256), F32),
+            pltpu.VMEM((960, 64), F32),
+            pltpu.VMEM((3, 15, 64), F32),
+            pltpu.VMEM((8, 8), jnp.int32),
+            pltpu.SMEM((8,), jnp.int32),
+            pltpu.VMEM((8, 15), jnp.int32),
+            pltpu.SMEM((15,), jnp.int32),
+            pltpu.VMEM((8, 256), jnp.int32),
+            pltpu.SMEM((256,), jnp.int32),
             dma((14,)),
             dma((2,)), dma((2,)), dma((2,)), dma((2,)),
             dma((16,)), dma((16,)), dma((4,)), dma((4,)), dma((4,)), dma((4,)),
         ],
         compiler_params=pltpu.CompilerParams(
-            collective_id=0, has_side_effects=True, vmem_limit_bytes=48 * 2**20
+            collective_id=0, has_side_effects=True, vmem_limit_bytes=60 * 2**20
         ),
     )(
-        rs, pts, basis.reshape(512, 256), transfer.reshape(960, 64), skel, near_list, near_count, inter_list,
-        inter_count, up_t, up_s, up_list, up_count,
+        rs, pts, basis.reshape(512, 256), transfer.reshape(960, 64), skel.transpose(1, 0, 2), near_list, near_count,
+        inter_list.T, inter_count, up_t.transpose(1, 2, 0).reshape(4096, 256), up_s.transpose(1, 2, 0).reshape(192, 256),
+        up_list.T, up_count,
     )
 
 

time: 48.6 us -> 38 us (0.78)
  local copies, waits for them, and re-layouts: 13.5 us -> 1.67 us
  Pallas kernels: 34.1 us -> 35.5 us
    unnamed x22 -> x1, local copies, waits for them, and re-layouts: 13.5 us -> 1.67 us
    pallas_call x1, Pallas kernels: 34.1 us -> 35.5 us  [on_device(): pl.pallas_call(kernel, out_shape=jax.ShapeDtypeStruct((32, 2048), F32), i...]
where the time goes in v1:
time: 38 us; the launch traced here: 37.2 us
  Pallas kernels  35.5 us (93%)
  local copies, waits for them, and re-layouts  1.67 us (4%)
    pallas_call x1, Pallas kernels, on_device(): pl.pallas_call(kernel, out_shape=jax.ShapeDtypeStruct((32, 2048), F32), i...  35.5 us
    unnamed x1, local copies, waits for them, and re-layouts  1.67 us

profile of v1, /device:TPU:2, one launch (start us, length us, event | category | flops | bytes accessed | tf_op | source)
XLA Modules:
  0.0 37.2 jit_solution(2831142776852192173)
XLA Ops:
  0.0 35.5 %shard_map.127 = f32[32,2048]{1,0:T(8,128)} custom-call(f32[32,2048]{1,0:T(8,128)} %rs.1, f32[3,2048]{1,0:T(4,128)} %pts_in.1, f32[512,256]{1,0:T(8,128)} %bitcast.12, f32[960,64]{1,0:T(8,128)} %bitcast.13, f32[3,15,64]{2,1,0:T(8,128)} %bitcast.15, s32[8,8]{1,0:T(8,128)} %near_list_in.1, s32[8]{0:T(128)} %near_count_in.1, s32[8,15]{1,0:T(8,128)} %bitcast.17, ...), custom_call_target="tpu_custom_call" | custom-call | tf_op jit(solution)/shard_map/pallas_call | solution.py:529
  35.5 1.7 %copy.15 = f32[32,2048]{1,0:T(8,128)} copy(f32[32,2048]{1,0:T(8,128)} %shard_map.127) | data formatting | bytes 524288

commit v2 on v1

--- a/solution.py
+++ b/solution.py
@@ -118,7 +118,7 @@
     rs, pts_in, basis_in, transfer_in, skel_in, near_list_in, near_count_in, inter_list_in, inter_count_in,
     up_t, up_s, up_list_in, up_count_in, out,
     xe, acc, f, ft, t2, bb_h, bb_l, bl_h, bl_l, bu_h, bu_l,
-    ce, lh, rh, ftl, ev, et, sv, st, su, fu, tu, zbuf, gc, tc, qh, ql,
+    ce, lh, rh, ftl, ev, et, sv, st, su, fu, tu, ftu, zbuf, gc, tc, qh, ql,
     pts, basis, transfer, skel, near_list, near_count, inter_list, inter_count, up_list, up_count,
     in_sem, near_send, near_recv, coef_send, coef_recv, z_send, z_recv, y_send, y_recv, x_send, x_recv,
 ):
@@ -273,7 +273,7 @@
     f[...] = tgt
     ft[1024:3072, :] = as_rows(src)
 
-    def near_leaf(t, first, last):
+    def near_leaf(t, first, last, between):
         targets = f[:, t * 256 : t * 256 + 256]
         total = jnp.zeros((32, 256), F32)
         for e in range(first, last):
@@ -282,77 +282,64 @@
             kh, kl = kern(dot(ft[part, :], targets))
             both = dot(jnp.concatenate([x_high, x_low], axis=0), kh)
             total += both[:32] + both[32:] + dot(x_high, kl)
+            between()
         return total
 
-    def own_leaf(t):
+    def spread(chores, blocks):
+        state = [0, 0]
+
+        def between():
+            state[0] += 1
+            until = len(chores) * state[0] // blocks
+            for chore in chores[state[1] : until]:
+                chore()
+            state[1] = until
+
+        return between
+
+    def own_leaf(t, between):
         part = slice(t * 256, t * 256 + 256)
         nugget = NUGGET * xe[0:32, t * 256 + 1024 : t * 256 + 1280]
-        acc[:, part] = nugget + near_leaf(t, max(t, 4), min(t + 9, 12))
-
-    with jax.named_scope("near_a"):
-        for t in range(4):
-            own_leaf(t)
+        acc[:, part] = nugget + near_leaf(t, max(t, 4), min(t + 9, 12), between)
 
     for load in loads[11:14]:
         load.wait()
 
-    with jax.named_scope("upper_weights"):
-        def turn(i, _):
-            half, k = lax.div(i, 32), lax.rem(i, 32)
-            first = pl.multiple_of(half * 4096 + k * 64, 64)
-            block = jnp.concatenate([ev[pl.ds(first, 64), :], ev[pl.ds(first + 2048, 64), :]], axis=0)
-            et[pl.ds(pl.multiple_of(i * 128, 128), 128), :] = block.T
-            return 0
-
-        lax.fori_loop(0, 64, turn, 0, unroll=4)
-
-        def edge(h, half):
-            two = et[pl.ds(half * 4096 + h - (128 if half == 0 else 0), 32, stride=128), :]
-            other = pltpu.roll(two, 64, 1)
-            low = low_lanes(32)
-            return jnp.concatenate([jnp.where(low, two, other), jnp.where(low, other, two)], axis=0)
-
-        nodes = (
-            (128 + 32 * g + 8 * y, 0, 0),
-            (132 + 32 * g + 8 * y, 0, 256),
-            (64 + 16 * g + 4 * y, 1, 512),
-            (16 + 4 * g, 1, 896),
-            (4, 1, 1280),
-        )
-        low64 = low_lanes(64)
-        for first, half, to in nodes:
-            for n in range(4):
-                keep = low64 if n < 2 else jnp.logical_not(low64)
-                put(bu_h, bu_l, to + n * 64, jnp.where(keep, edge(first + n, half), 0.0))
-        for first, to in ((32 + 8 * g + 2 * y, 768), (8 + 2 * g, 1152)):
-            for n in range(2):
-                put(bu_h, bu_l, to + n * 64, edge(first + n, 1))
-    with jax.named_scope("upper_skeletons"):
-        su[...] = jnp.zeros((8, 4352), F32)
-        for c in range(3):
-            for h in range(2):
-                first = h * 128
-                block = jnp.concatenate([sv[c * 64 : c * 64 + 64, first : first + 128]] * 2, axis=0)
-                st[c, first : first + 128, :] = block.T
-        at_lane = 0
-        for first, n in zip(firsts, UPPER):
-            for i in range(n // 2):
-                one, two = st[:, pl.ds(first + 2 * i, 1), :], st[:, pl.ds(first + 2 * i + 1, 1), :]
-                pair = jnp.where(lax.broadcasted_iota(jnp.int32, (3, 1, 128), 2) < 64, one, two)
-                su[0:3, at_lane : at_lane + 128] = scaled(pair.reshape(3, 128))
-                at_lane += 128
-        fu[...] = features(su[...], "t")[0]
-        heap = [lax.div(256 + dev, 2 ** (i + 1)) for i in range(7)]
-        tu[...] = jnp.zeros((8, 512), F32)
-        for i, (m, n) in enumerate(((0, 1), (2, 3), (4, 5), (6, 6))):
-            one, two = st[:, pl.ds(heap[m], 1), :], st[:, pl.ds(heap[n], 1), :]
-            pair = jnp.where(lax.broadcasted_iota(jnp.int32, (3, 1, 128), 2) < 64, one, two)
-            tu[0:3, i * 128 : i * 128 + 128] = scaled(pair.reshape(3, 128))
-        ftu = as_rows(features(tu[...], "s")[0])
-
-    with jax.named_scope("near_b"):
-        for t in range(4, 8):
-            own_leaf(t)
+    def turn(i):
+        first = i // 32 * 4096 + i % 32 * 64
+        block = jnp.concatenate([ev[first : first + 64, :], ev[first + 2048 : first + 2112, :]], axis=0)
+        et[i * 128 : i * 128 + 128, :] = block.T
+
+    def edge(h, half):
+        two = et[pl.ds(half * 4096 + h - (128 if half == 0 else 0), 32, stride=128), :]
+        other = pltpu.roll(two, 64, 1)
+        low = low_lanes(32)
+        return jnp.concatenate([jnp.where(low, two, other), jnp.where(low, other, two)], axis=0)
+
+    low64 = low_lanes(64)
+
+    def put_edge(h, half, to, keep):
+        value = edge(h, half)
+        put(bu_h, bu_l, to, value if keep is None else jnp.where(keep, value, 0.0))
+
+    nodes = (
+        (128 + 32 * g + 8 * y, 0, 0),
+        (132 + 32 * g + 8 * y, 0, 256),
+        (64 + 16 * g + 4 * y, 1, 512),
+        (16 + 4 * g, 1, 896),
+        (4, 1, 1280),
+    )
+    chores = [functools.partial(turn, i) for i in range(64)]
+    for first, half, to in nodes:
+        for n in range(4):
+            keep = low64 if n < 2 else jnp.logical_not(low64)
+            chores.append(functools.partial(put_edge, first + n, half, to + n * 64, keep))
+    for first, to in ((32 + 8 * g + 2 * y, 768), (8 + 2 * g, 1152)):
+        for n in range(2):
+            chores.append(functools.partial(put_edge, first + n, 1, to + n * 64, None))
+    between = spread(chores, 26)
+    for t in range(4):
+        own_leaf(t, between)
 
     def take_row(k, _):
         row_copy(k, False).wait_recv()
@@ -385,15 +372,49 @@
     for k in range(1, 4):
         plane_copy(k, True).start()
 
-    for copy in near_copies:
-        copy.wait_recv()
-    with jax.named_scope("near_c"):
-        src = features(xe[32:40, 0:1024], "s")[0]
-        ft[0:1024, :] = as_rows(src)
-        src = features(xe[32:40, 3072:4096], "s")[0]
-        ft[3072:4096, :] = as_rows(src)
-        for t in range(4):
-            acc[:, t * 256 : t * 256 + 256] += near_leaf(t, t, 4)
+    heap = [lax.div(256 + dev, 2 ** (i + 1)) for i in range(7)]
+    low3 = lax.broadcasted_iota(jnp.int32, (3, 1, 128), 2) < 64
+
+    def turn_skeleton(c, h):
+        block = jnp.concatenate([sv[c * 64 : c * 64 + 64, h * 128 : h * 128 + 128]] * 2, axis=0)
+        st[c, h * 128 : h * 128 + 128, :] = block.T
+
+    def put_skeletons(ref, m, n, at_lane):
+        pair = jnp.where(low3, st[:, pl.ds(m, 1), :], st[:, pl.ds(n, 1), :])
+        ref[0:3, at_lane : at_lane + 128] = scaled(pair.reshape(3, 128))
+
+    def put_features():
+        fu[...] = features(su[...], "t")[0]
+        ftu[...] = as_rows(features(tu[...], "s")[0])
+
+    last = [jnp.concatenate([root_e, root_e], axis=0)]
+
+    def path_product(i):
+        if i > 0:
+            last[0] = matmul(last[0], *halves(edge(heap[i - 1], 0 if i == 1 else 1)[:, 0:64]))
+        qh[i], ql[i] = halves(last[0])
+
+    su[...] = jnp.zeros((8, 4352), F32)
+    tu[...] = jnp.zeros((8, 512), F32)
+    skeletons = [functools.partial(turn_skeleton, c, h) for c in range(3) for h in range(2)]
+    at_lane = 0
+    for first, n in zip(firsts, UPPER):
+        for i in range(n // 2):
+            skeletons.append(functools.partial(put_skeletons, su, first + 2 * i, first + 2 * i + 1, at_lane))
+            at_lane += 128
+    for i, (m, n) in enumerate(((0, 1), (2, 3), (4, 5), (6, 6))):
+        skeletons.append(functools.partial(put_skeletons, tu, heap[m], heap[n], i * 128))
+    skeletons.append(put_features)
+    products = [functools.partial(path_product, i) for i in range(7)]
+    chores = []
+    for i, chore in enumerate(skeletons):
+        chores.append(chore)
+        if i % 6 == 5 and products:
+            chores.append(products.pop(0))
+    chores += products
+    between = spread(chores, 26)
+    for t in range(4, 8):
+        own_leaf(t, between)
 
     for k in range(1, 4):
         plane_copy(k, False).wait_recv()
@@ -415,12 +436,12 @@
     for k in range(1, 4):
         group_copy(k, True).start()
 
-    with jax.named_scope("near_d"):
-        for t in range(4, 8):
-            acc[:, t * 256 : t * 256 + 256] += near_leaf(t, 12, t + 9)
-
-    for copy in coef_copies:
+    for copy in near_copies + coef_copies:
         copy.wait_recv()
+    src = features(xe[32:40, 0:1024], "s")[0]
+    ft[0:1024, :] = as_rows(src)
+    src = features(xe[32:40, 3072:4096], "s")[0]
+    ft[3072:4096, :] = as_rows(src)
     ftl[...] = as_rows(features(ce[32:40, :], "s")[0])
     spot = lax.broadcasted_iota(jnp.int32, (8, 15), 1)
     slot = lax.broadcasted_iota(jnp.int32, (8, 15), 0)
@@ -432,62 +453,79 @@
     def listed(n, ids):
         return jnp.sum(jnp.where(inter[:, n : n + 1] == ids, 1.0, 0.0), axis=0, keepdims=True)
 
-    table = jnp.concatenate([lh[:, 384:640], ce[:, 0:256], ce[:, 768:1024], rh[:, 0:256]], axis=1)
-    feats = features(table[32:40], "t")[0]
-    ids = lanes(1024) // 64 + (dev * 8 - 4)
-    field0 = []
-    for j, at_lane in enumerate((0, 128, 768, 896)):
-        part = slice(j * 128, j * 128 + 640)
-        masks = [listed(2 * j, ids[:, part]), listed(2 * j + 1, ids[:, part])]
-        field0.append(beside(couple(ftl[at_lane : at_lane + 128, :], feats[:, part], table[0:32, part], masks)))
-    table = jnp.concatenate([lh[:, 256:384], ce[:, 256:384], ce[:, 640:768], rh[:, 256:384]], axis=1)
-    feats = features(table[32:40], "t")[0]
-    ids = lanes(512) // 64 + (dev * 4 - 2)
-    field1 = []
-    for j, at_lane in enumerate((256, 640)):
-        part = slice(j * 128, j * 128 + 384)
-        masks = [listed(8 + 2 * j, ids[:, part]), listed(9 + 2 * j, ids[:, part])]
-        field1.append(beside(couple(ftl[at_lane : at_lane + 128, :], feats[:, part], table[0:32, part], masks)))
-    table = jnp.concatenate([lh[:, 0:128], ce[:, 384:512], rh[:, 384:512]], axis=1)
-    feats = features(table[32:40], "t")[0]
-    ids = lanes(384) // 64 + (dev * 2 - 2)
-    field2 = beside(couple(ftl[384:512, :], feats, table[0:32], [listed(12, ids), listed(13, ids)]))
-    table = jnp.concatenate([lh[:, 128:256], ce[:, 512:640], rh[:, 512:640]], axis=1)
-    feats = features(table[32:40], "t")[0]
-    spot = lanes(384)
-    ids = jnp.where(lax.rem(spot, 128) < 64, spot // 128 + (dev - 1), -1)
-    found = listed(14, ids)
-    field3 = beside(couple(ftl[512:640, :], feats, table[0:32], [found, found]))
-
-    product = jnp.concatenate([root_e, root_e], axis=0)
-    for i in range(7):
-        if i > 0:
-            product = matmul(product, *halves(edge(heap[i - 1], 0 if i == 1 else 1)[:, 0:64]))
-        qh[i], ql[i] = halves(product)
+    one_ids = jnp.where(lax.rem(lanes(384), 128) < 64, lanes(384) // 128 + (dev - 1), -1)
+    tables = (
+        ([lh[:, 384:640], ce[:, 0:256], ce[:, 768:1024], rh[:, 0:256]], lanes(1024) // 64 + (dev * 8 - 4)),
+        ([lh[:, 256:384], ce[:, 256:384], ce[:, 640:768], rh[:, 256:384]], lanes(512) // 64 + (dev * 4 - 2)),
+        ([lh[:, 0:128], ce[:, 384:512], rh[:, 384:512]], lanes(384) // 64 + (dev * 2 - 2)),
+        ([lh[:, 128:256], ce[:, 512:640], rh[:, 512:640]], one_ids),
+    )
+    tables = [(jnp.concatenate(parts, axis=1), ids) for parts, ids in tables]
+    tables = [(table[0:32], features(table[32:40], "t")[0], ids) for table, ids in tables]
+    fields = {}
+
+    def local_field(level, m, n, at_lane, first, width):
+        coefs, feats, ids = tables[level]
+        part = slice(first, first + width)
+        masks = [listed(m, ids[:, part]), listed(n, ids[:, part])]
+        fields[at_lane] = beside(couple(ftl[at_lane : at_lane + 128, :], feats[:, part], coefs[:, part], masks))
+
     node = lax.broadcasted_iota(jnp.int32, (8, 256), 1)
     up_slots = lax.broadcasted_iota(jnp.int32, (8, 1), 0)
     up_lists = up_list[...].astype(F32)
-
-    def path_field(i, coefs):
-        h = heap[i]
+    path = {}
+
+    def path_kernel(i):
         first, n = sum(UPPER[:i]) * 64, UPPER[i] * 64
-        column = jnp.sum(jnp.where(node == h, up_lists, 0.0), axis=1, keepdims=True)
-        column = jnp.where(up_slots < up_count[h], column, -1000.0)
+        column = jnp.sum(jnp.where(node == heap[i], up_lists, 0.0), axis=1, keepdims=True)
+        column = jnp.where(up_slots < up_count[heap[i]], column, -1000.0)
         ids = (lanes(n) // 64 + firsts[i]).astype(F32)
         found = jnp.sum(jnp.where(column == ids, 1.0, 0.0), axis=0, keepdims=True)
-        field = couple(ftu[i * 64 : i * 64 + 64, :], fu[:, first : first + n], coefs, [found])
-        return matmul(field, qh[i], ql[i], NT)
-
-    incoming = path_field(0, jnp.concatenate([gc[k, :, 0:512] for k in range(4)], axis=1))
-    incoming += path_field(1, jnp.concatenate([gc[k, :, 512:768] for k in range(4)], axis=1))
-    incoming += path_field(2, jnp.concatenate([gc[k, :, 768:896] for k in range(4)], axis=1))
-    incoming += path_field(3, jnp.concatenate(level4, axis=1))
-    incoming += path_field(4, level3)
+        path[i] = (found * KAPPA, *kern(dot(ftu[i * 64 : i * 64 + 64, :], fu[:, first : first + n])))
+
+    def path_field(i, coefs):
+        found, kh, kl = path[i]
+        return matmul(matmul(coefs * found, kh, kl, NT), qh[i], ql[i], NT)
+
+    incoming = []
+
+    def path_step(i, coefs):
+        path_kernel(i)
+        incoming.append(path_field(i, coefs()))
+
+    def group_lanes(first, last):
+        return lambda: jnp.concatenate([gc[k, :, first:last] for k in range(4)], axis=1)
+
+    chores = [
+        functools.partial(path_kernel, 5),
+        functools.partial(path_kernel, 6),
+        functools.partial(path_step, 0, group_lanes(0, 512)),
+        functools.partial(path_step, 1, group_lanes(512, 768)),
+        functools.partial(path_step, 2, group_lanes(768, 896)),
+        functools.partial(path_step, 3, lambda: jnp.concatenate(level4, axis=1)),
+        functools.partial(path_step, 4, lambda: level3),
+        functools.partial(local_field, 3, 14, 14, 512, 0, 384),
+        functools.partial(local_field, 2, 12, 13, 384, 0, 384),
+        functools.partial(local_field, 1, 8, 9, 256, 0, 384),
+        functools.partial(local_field, 1, 10, 11, 640, 128, 384),
+    ]
+    for j, at_lane in enumerate((0, 128, 768, 896)):
+        chores.append(functools.partial(local_field, 0, 2 * j, 2 * j + 1, at_lane, j * 128, 640))
+    between = spread(chores, 20)
+    for t in range(4):
+        acc[:, t * 256 : t * 256 + 256] += near_leaf(t, t, 4, between)
+    for t in range(4, 8):
+        acc[:, t * 256 : t * 256 + 256] += near_leaf(t, 12, t + 9, between)
+
     for k in range(1, 4):
         group_copy(k, False).wait_recv()
     level2 = [jnp.where(low32, tc[0], tc[1]), jnp.where(low32, tc[2], tc[3])]
-    incoming += path_field(5, jnp.concatenate(level2, axis=1))
-    incoming += path_field(6, lift(level2, bu_h, bu_l, 1280))
+    incoming.append(path_field(5, jnp.concatenate(level2, axis=1)))
+    incoming.append(path_field(6, lift(level2, bu_h, bu_l, 1280)))
+    incoming = sum(incoming[1:], incoming[0])
+    field0 = [fields[0], fields[128], fields[768], fields[896]]
+    field1 = [fields[256], fields[640]]
+    field2, field3 = fields[384], fields[512]
 
     def lower(value, first, n):
         return matmul(value, bl_h[first : first + n, :], bl_l[first : first + n, :], NT)
@@ -554,6 +592,7 @@
             pltpu.VMEM((8, 4352), F32),
             pltpu.VMEM((FEATS, 4352), BF16),
             pltpu.VMEM((8, 512), F32),
+            pltpu.VMEM((512, FEATS), BF16),
             pltpu.VMEM((16, 16, 128), F32),
             pltpu.VMEM((4, 32, 1024), F32),
             pltpu.VMEM((4, 32, 128), F32),

time: 38 us -> 36.2 us (0.953)
  the two profiles are of different devices: /device:TPU:2 before, /device:TPU:1 now
where the time goes in v2:
time: 36.2 us; the launch traced here: 36.1 us
  Pallas kernels  34.4 us (95%)
  local copies, waits for them, and re-layouts  1.67 us (5%)
    pallas_call x1, Pallas kernels, on_device(): pl.pallas_call(kernel, out_shape=jax.ShapeDtypeStruct((32, 2048), F32), i...  34.4 us
    unnamed x1, local copies, waits for them, and re-layouts  1.67 us

profile of v2, /device:TPU:1, one launch (start us, length us, event | category | flops | bytes accessed | tf_op | source)
XLA Modules:
  0.0 36.1 jit_solution(15397009574168932046)
XLA Ops:
  0.0 34.4 %shard_map.127 = f32[32,2048]{1,0:T(8,128)} custom-call(f32[32,2048]{1,0:T(8,128)} %rs.1, f32[3,2048]{1,0:T(4,128)} %pts_in.1, f32[512,256]{1,0:T(8,128)} %bitcast.12, f32[960,64]{1,0:T(8,128)} %bitcast.13, f32[3,15,64]{2,1,0:T(8,128)} %bitcast.15, s32[8,8]{1,0:T(8,128)} %near_list_in.1, s32[8]{0:T(128)} %near_count_in.1, s32[8,15]{1,0:T(8,128)} %bitcast.17, ...), custom_call_target="tpu_custom_call" | custom-call | tf_op jit(solution)/shard_map/pallas_call | solution.py:567
  34.4 1.7 %copy.15 = f32[32,2048]{1,0:T(8,128)} copy(f32[32,2048]{1,0:T(8,128)} %shard_map.127) | data formatting | bytes 524288

commit v3 on v2

--- a/solution.py
+++ b/solution.py
@@ -118,15 +118,17 @@
     rs, pts_in, basis_in, transfer_in, skel_in, near_list_in, near_count_in, inter_list_in, inter_count_in,
     up_t, up_s, up_list_in, up_count_in, out,
     xe, acc, f, ft, t2, bb_h, bb_l, bl_h, bl_l, bu_h, bu_l,
-    ce, lh, rh, ftl, ev, et, sv, st, su, fu, tu, ftu, zbuf, gc, tc, qh, ql,
+    ce, lh, rh, ftl, ev, et, sv, st, su, fu, tu, ftu, mine, other, zbuf, gc, hc, tc, qh, ql,
     pts, basis, transfer, skel, near_list, near_count, inter_list, inter_count, up_list, up_count,
-    in_sem, near_send, near_recv, coef_send, coef_recv, z_send, z_recv, y_send, y_recv, x_send, x_recv,
+    in_sem, near_send, near_recv, coef_send, coef_recv, c_send, c_recv, z_send, z_recv, h_send, h_recv,
+    y_send, y_recv, x_send, x_recv,
 ):
     g = lax.axis_index("group")
     b = lax.axis_index("bulk")
     z = lax.rem(lax.div(b, 2), 8)
     y = lax.div(b, 16)
     r = lax.rem(b, 16)
+    core = lax.rem(b, 2)
     dev = g * 64 + b
 
     def at(d):
@@ -164,11 +166,14 @@
     greet(right)
     greet(left)
 
-    def greet_row(k, _):
-        greet((g, y * 16 + lax.rem(r + k, 16)))
-        return 0
-
-    lax.fori_loop(1, 16, greet_row, 0)
+    partner = (g, b + 1 - 2 * core)
+    greet(partner)
+
+    def along_z(k):
+        return lax.rem(z + k, 8)
+
+    for k in range(1, 8):
+        greet((g, y * 16 + along_z(k) * 2 + core))
     for k in range(1, 4):
         greet((g, lax.rem(y + k, 4) * 16 + r))
         greet((lax.rem(g + k, 4), b))
@@ -182,7 +187,7 @@
     for i, (m, n) in enumerate(order):
         ce[32:35, i * 128 : i * 128 + 128] = scaled(jnp.concatenate([skel[:, m, :], skel[:, n, :]], axis=1))
     loads[0].wait()
-    pl.semaphore_wait(barrier, 23)
+    pl.semaphore_wait(barrier, 16)
 
     near_copies = [
         pltpu.make_async_remote_copy(
@@ -194,8 +199,6 @@
             device_id=left, device_id_type=MESH,
         ),
     ]
-    for copy in near_copies:
-        copy.start()
 
     loads[3].wait()
     loads[4].wait()
@@ -235,21 +238,11 @@
     top = lift([mid_a, mid_b], bl_h, bl_l, 512)
     root = lift([top], bl_h, bl_l, 768)
     term = lift([root[:, 0:64]], bl_h, bl_l, 896)
-    zbuf[r] = jnp.where(low_lanes(16), term[0:16], term[16:32])
-
-    def row_copy(k, sender):
-        to = lax.rem(r + k, 16)
-        slot = r if sender else to
-        return pltpu.make_async_remote_copy(
-            zbuf.at[slot], zbuf.at[slot], z_send.at[k], z_recv.at[slot],
-            device_id=(g, y * 16 + to), device_id_type=MESH,
-        )
-
-    def send_row(k, _):
-        row_copy(k, True).start()
-        return 0
-
-    lax.fori_loop(1, 16, send_row, 0)
+    mine[...] = jnp.where(low_lanes(16), term[0:16], term[16:32])
+    core_copy = pltpu.make_async_remote_copy(
+        mine, other, c_send, c_recv, device_id=partner, device_id_type=MESH
+    )
+    core_copy.start()
     for i, value in enumerate((leaf[0], leaf[1], mid_a, top, root, mid_b, leaf[2], leaf[3])):
         ce[0:32, i * 128 : i * 128 + 128] = value
     coef_copies = [
@@ -260,9 +253,6 @@
             ce.at[:, 0:640], rh, coef_send.at[1], coef_recv.at[1], device_id=left, device_id_type=MESH
         ),
     ]
-    for copy in coef_copies:
-        copy.start()
-
     for load in loads[5:11]:
         load.wait()
     near = usable(near_list[...], counted(near_count, 8, 8))
@@ -272,6 +262,21 @@
     src, tgt = features(xe[32:40, 1024:3072])
     f[...] = tgt
     ft[1024:3072, :] = as_rows(src)
+
+    core_copy.wait_recv()
+    zbuf[z] = mine[...] + other[...]
+
+    def row_copy(k, sender):
+        slot = z if sender else along_z(k)
+        return pltpu.make_async_remote_copy(
+            zbuf.at[slot], zbuf.at[slot], z_send.at[k], z_recv.at[slot],
+            device_id=(g, y * 16 + along_z(k) * 2 + core), device_id_type=MESH,
+        )
+
+    for k in (4, 3, 5, 2, 6, 1, 7):
+        row_copy(k, True).start()
+    for copy in coef_copies:
+        copy.start()
 
     def near_leaf(t, first, last, between):
         targets = f[:, t * 256 : t * 256 + 256]
@@ -337,20 +342,16 @@
     for first, to in ((32 + 8 * g + 2 * y, 768), (8 + 2 * g, 1152)):
         for n in range(2):
             chores.append(functools.partial(put_edge, first + n, 1, to + n * 64, None))
-    between = spread(chores, 26)
-    for t in range(4):
+    between = spread(chores, 18)
+    for t in range(3):
         own_leaf(t, between)
 
-    def take_row(k, _):
+    for k in range(1, 8):
         row_copy(k, False).wait_recv()
-        return 0
-
-    lax.fori_loop(1, 16, take_row, 0)
     low16 = low_lanes(16)
     level7 = []
     for j in range(4):
-        one = zbuf[4 * j] + zbuf[4 * j + 1]
-        two = zbuf[4 * j + 2] + zbuf[4 * j + 3]
+        one, two = zbuf[2 * j], zbuf[2 * j + 1]
         level7.append(
             jnp.concatenate(
                 [jnp.where(low16, one, pltpu.roll(two, 64, 1)), jnp.where(low16, pltpu.roll(one, 64, 1), two)], axis=0
@@ -359,7 +360,18 @@
     level6 = [lift(level7[0:2], bu_h, bu_l, 0), lift(level7[2:4], bu_h, bu_l, 256)]
     level5 = lift(level6, bu_h, bu_l, 512)
     level4 = lift([level5], bu_h, bu_l, 768)
-    for i, value in enumerate((*level7, *level6, level5, level4)):
+    hc[y] = level4
+
+    def fourth_copy(k, sender):
+        to = lax.rem(y + k, 4)
+        slot = y if sender else to
+        return pltpu.make_async_remote_copy(
+            hc.at[slot], hc.at[slot], h_send.at[k], h_recv.at[slot], device_id=(g, to * 16 + r), device_id_type=MESH
+        )
+
+    for k in (2, 1, 3):
+        fourth_copy(k, True).start()
+    for i, value in enumerate((*level7, *level6, level5)):
         gc[y, :, i * 128 : i * 128 + 128] = value
 
     def plane_copy(k, sender):
@@ -369,8 +381,10 @@
             gc.at[slot], gc.at[slot], y_send.at[k], y_recv.at[slot], device_id=(g, to * 16 + r), device_id_type=MESH
         )
 
-    for k in range(1, 4):
+    for k in (2, 1, 3):
         plane_copy(k, True).start()
+    for copy in near_copies:
+        copy.start()
 
     heap = [lax.div(256 + dev, 2 ** (i + 1)) for i in range(7)]
     low3 = lax.broadcasted_iota(jnp.int32, (3, 1, 128), 2) < 64
@@ -412,16 +426,16 @@
         if i % 6 == 5 and products:
             chores.append(products.pop(0))
     chores += products
-    between = spread(chores, 26)
-    for t in range(4, 8):
+    between = spread(chores, 16)
+    for t in range(3, 5):
         own_leaf(t, between)
 
     for k in range(1, 4):
-        plane_copy(k, False).wait_recv()
+        fourth_copy(k, False).wait_recv()
     low32 = low_lanes(32)
     level4 = [
-        jnp.where(low32, gc[0, :, 896:1024], gc[1, :, 896:1024]),
-        jnp.where(low32, gc[2, :, 896:1024], gc[3, :, 896:1024]),
+        jnp.where(low32, hc[0], hc[1]),
+        jnp.where(low32, hc[2], hc[3]),
     ]
     level3 = lift(level4, bu_h, bu_l, 896)
     tc[g] = lift([level3], bu_h, bu_l, 1152)
@@ -496,12 +510,7 @@
     def group_lanes(first, last):
         return lambda: jnp.concatenate([gc[k, :, first:last] for k in range(4)], axis=1)
 
-    chores = [
-        functools.partial(path_kernel, 5),
-        functools.partial(path_kernel, 6),
-        functools.partial(path_step, 0, group_lanes(0, 512)),
-        functools.partial(path_step, 1, group_lanes(512, 768)),
-        functools.partial(path_step, 2, group_lanes(768, 896)),
+    chores = [functools.partial(path_kernel, i) for i in (5, 6, 0, 1, 2)] + [
         functools.partial(path_step, 3, lambda: jnp.concatenate(level4, axis=1)),
         functools.partial(path_step, 4, lambda: level3),
         functools.partial(local_field, 3, 14, 14, 512, 0, 384),
@@ -511,7 +520,9 @@
     ]
     for j, at_lane in enumerate((0, 128, 768, 896)):
         chores.append(functools.partial(local_field, 0, 2 * j, 2 * j + 1, at_lane, j * 128, 640))
-    between = spread(chores, 20)
+    between = spread(chores, 38)
+    for t in range(5, 8):
+        own_leaf(t, between)
     for t in range(4):
         acc[:, t * 256 : t * 256 + 256] += near_leaf(t, t, 4, between)
     for t in range(4, 8):
@@ -520,8 +531,14 @@
     for k in range(1, 4):
         group_copy(k, False).wait_recv()
     level2 = [jnp.where(low32, tc[0], tc[1]), jnp.where(low32, tc[2], tc[3])]
+    level1 = lift(level2, bu_h, bu_l, 1280)
+    for k in range(1, 4):
+        plane_copy(k, False).wait_recv()
     incoming.append(path_field(5, jnp.concatenate(level2, axis=1)))
-    incoming.append(path_field(6, lift(level2, bu_h, bu_l, 1280)))
+    incoming.append(path_field(6, level1))
+    incoming.append(path_field(0, group_lanes(0, 512)()))
+    incoming.append(path_field(1, group_lanes(512, 768)()))
+    incoming.append(path_field(2, group_lanes(768, 896)()))
     incoming = sum(incoming[1:], incoming[0])
     field0 = [fields[0], fields[128], fields[768], fields[896]]
     field1 = [fields[256], fields[640]]
@@ -548,12 +565,11 @@
     for copy in near_copies + coef_copies:
         copy.wait_send()
 
-    def sent_row(k, _):
+    core_copy.wait_send()
+    for k in range(1, 8):
         row_copy(k, True).wait_send()
-        return 0
-
-    lax.fori_loop(1, 16, sent_row, 0)
     for k in range(1, 4):
+        fourth_copy(k, True).wait_send()
         plane_copy(k, True).wait_send()
         group_copy(k, True).wait_send()
 
@@ -593,8 +609,11 @@
             pltpu.VMEM((FEATS, 4352), BF16),
             pltpu.VMEM((8, 512), F32),
             pltpu.VMEM((512, FEATS), BF16),
-            pltpu.VMEM((16, 16, 128), F32),
-            pltpu.VMEM((4, 32, 1024), F32),
+            pltpu.VMEM((16, 128), F32),
+            pltpu.VMEM((16, 128), F32),
+            pltpu.VMEM((8, 16, 128), F32),
+            pltpu.VMEM((4, 32, 896), F32),
+            pltpu.VMEM((4, 32, 128), F32),
             pltpu.VMEM((4, 32, 128), F32),
             pltpu.VMEM((7, 128, 64), BF16),
             pltpu.VMEM((7, 128, 64), BF16),
@@ -610,10 +629,10 @@
             pltpu.SMEM((256,), jnp.int32),
             dma((14,)),
             dma((2,)), dma((2,)), dma((2,)), dma((2,)),
-            dma((16,)), dma((16,)), dma((4,)), dma((4,)), dma((4,)), dma((4,)),
+            dma, dma, dma((8,)), dma((8,)), dma((4,)), dma((4,)), dma((4,)), dma((4,)), dma((4,)), dma((4,)),
         ],
         compiler_params=pltpu.CompilerParams(
-            collective_id=0, has_side_effects=True, vmem_limit_bytes=60 * 2**20
+            collective_id=0, has_side_effects=True, vmem_limit_bytes=58 * 2**20
         ),
     )(
         rs, pts, basis.reshape(512, 256), transfer.reshape(960, 64), skel.transpose(1, 0, 2), near_list, near_count,

time: 36.2 us -> 34.8 us (0.961)
  the two profiles are of different devices: /device:TPU:1 before, /device:TPU:2 now
where the time goes in v3:
time: 34.8 us; the launch traced here: 34.5 us
  Pallas kernels  32.8 us (94%)
  local copies, waits for them, and re-layouts  1.67 us (5%)
    pallas_call x1, Pallas kernels, on_device(): pl.pallas_call(kernel, out_shape=jax.ShapeDtypeStruct((32, 2048), F32), i...  32.8 us
    unnamed x1, local copies, waits for them, and re-layouts  1.67 us

profile of v3, /device:TPU:2, one launch (start us, length us, event | category | flops | bytes accessed | tf_op | source)
XLA Modules:
  0.0 34.5 jit_solution(18099462583241110225)
XLA Ops:
  0.0 32.8 %shard_map.127 = f32[32,2048]{1,0:T(8,128)} custom-call(f32[32,2048]{1,0:T(8,128)} %rs.1, f32[3,2048]{1,0:T(4,128)} %pts_in.1, f32[512,256]{1,0:T(8,128)} %bitcast.12, f32[960,64]{1,0:T(8,128)} %bitcast.13, f32[3,15,64]{2,1,0:T(8,128)} %bitcast.15, s32[8,8]{1,0:T(8,128)} %near_list_in.1, s32[8]{0:T(128)} %near_count_in.1, s32[8,15]{1,0:T(8,128)} %bitcast.17, ...), custom_call_target="tpu_custom_call" | custom-call | tf_op jit(solution)/shard_map/pallas_call | solution.py:583
  32.9 1.7 %copy.15 = f32[32,2048]{1,0:T(8,128)} copy(f32[32,2048]{1,0:T(8,128)} %shard_map.127) | data formatting | bytes 524288

commit v4 on v3

--- a/solution.py
+++ b/solution.py
@@ -187,7 +187,6 @@
     for i, (m, n) in enumerate(order):
         ce[32:35, i * 128 : i * 128 + 128] = scaled(jnp.concatenate([skel[:, m, :], skel[:, n, :]], axis=1))
     loads[0].wait()
-    pl.semaphore_wait(barrier, 16)
 
     near_copies = [
         pltpu.make_async_remote_copy(
@@ -242,6 +241,7 @@
     core_copy = pltpu.make_async_remote_copy(
         mine, other, c_send, c_recv, device_id=partner, device_id_type=MESH
     )
+    pl.semaphore_wait(barrier, 16)
     core_copy.start()
     for i, value in enumerate((leaf[0], leaf[1], mid_a, top, root, mid_b, leaf[2], leaf[3])):
         ce[0:32, i * 128 : i * 128 + 128] = value
@@ -387,15 +387,16 @@
         copy.start()
 
     heap = [lax.div(256 + dev, 2 ** (i + 1)) for i in range(7)]
-    low3 = lax.broadcasted_iota(jnp.int32, (3, 1, 128), 2) < 64
+    low1 = lanes(128) < 64
 
     def turn_skeleton(c, h):
         block = jnp.concatenate([sv[c * 64 : c * 64 + 64, h * 128 : h * 128 + 128]] * 2, axis=0)
         st[c, h * 128 : h * 128 + 128, :] = block.T
 
     def put_skeletons(ref, m, n, at_lane):
-        pair = jnp.where(low3, st[:, pl.ds(m, 1), :], st[:, pl.ds(n, 1), :])
-        ref[0:3, at_lane : at_lane + 128] = scaled(pair.reshape(3, 128))
+        for c in range(3):
+            pair = jnp.where(low1, st[c, pl.ds(m, 1), :], st[c, pl.ds(n, 1), :])
+            ref[c : c + 1, at_lane : at_lane + 128] = scaled(pair)
 
     def put_features():
         fu[...] = features(su[...], "t")[0]

time: 34.8 us -> 33.8 us (0.971)
  Pallas kernels: 32.8 us -> 32 us
    pallas_call x1, Pallas kernels: 32.8 us -> 32 us  [on_device(): pl.pallas_call(kernel, out_shape=jax.ShapeDtypeStruct((32, 2048), F32), i...]
where the time goes in v4:
time: 33.8 us; the launch traced here: 33.7 us
  Pallas kernels  32 us (95%)
  local copies, waits for them, and re-layouts  1.67 us (5%)
    pallas_call x1, Pallas kernels, on_device(): pl.pallas_call(kernel, out_shape=jax.ShapeDtypeStruct((32, 2048), F32), i...  32 us
    unnamed x1, local copies, waits for them, and re-layouts  1.67 us

profile of v4, /device:TPU:2, one launch (start us, length us, event | category | flops | bytes accessed | tf_op | source)
XLA Modules:
  0.0 33.7 jit_solution(13225754710698314464)
XLA Ops:
  0.0 32.0 %shard_map.127 = f32[32,2048]{1,0:T(8,128)} custom-call(f32[32,2048]{1,0:T(8,128)} %rs.1, f32[3,2048]{1,0:T(4,128)} %pts_in.1, f32[512,256]{1,0:T(8,128)} %bitcast.12, f32[960,64]{1,0:T(8,128)} %bitcast.13, f32[3,15,64]{2,1,0:T(8,128)} %bitcast.15, s32[8,8]{1,0:T(8,128)} %near_list_in.1, s32[8]{0:T(128)} %near_count_in.1, s32[8,15]{1,0:T(8,128)} %bitcast.17, ...), custom_call_target="tpu_custom_call" | custom-call | tf_op jit(solution)/shard_map/pallas_call | solution.py:584
  32.0 1.7 %copy.15 = f32[32,2048]{1,0:T(8,128)} copy(f32[32,2048]{1,0:T(8,128)} %shard_map.127) | data formatting | bytes 524288

commit v5 on v4

--- a/solution.py
+++ b/solution.py
@@ -342,8 +342,8 @@
     for first, to in ((32 + 8 * g + 2 * y, 768), (8 + 2 * g, 1152)):
         for n in range(2):
             chores.append(functools.partial(put_edge, first + n, 1, to + n * 64, None))
-    between = spread(chores, 18)
-    for t in range(3):
+    between = spread(chores, 26)
+    for t in range(4):
         own_leaf(t, between)
 
     for k in range(1, 8):
@@ -427,8 +427,8 @@
         if i % 6 == 5 and products:
             chores.append(products.pop(0))
     chores += products
-    between = spread(chores, 16)
-    for t in range(3, 5):
+    between = spread(chores, 15)
+    for t in range(4, 6):
         own_leaf(t, between)
 
     for k in range(1, 4):
@@ -521,8 +521,8 @@
     ]
     for j, at_lane in enumerate((0, 128, 768, 896)):
         chores.append(functools.partial(local_field, 0, 2 * j, 2 * j + 1, at_lane, j * 128, 640))
-    between = spread(chores, 38)
-    for t in range(5, 8):
+    between = spread(chores, 31)
+    for t in range(6, 8):
         own_leaf(t, between)
     for t in range(4):
         acc[:, t * 256 : t * 256 + 256] += near_leaf(t, t, 4, between)

time: 33.8 us -> 33.4 us (0.988)
  no operation moved by 1% of the time
where the time goes in v5:
time: 33.4 us; the launch traced here: 33.3 us
  Pallas kernels  31.7 us (95%)
  local copies, waits for them, and re-layouts  1.67 us (5%)
    pallas_call x1, Pallas kernels, on_device(): pl.pallas_call(kernel, out_shape=jax.ShapeDtypeStruct((32, 2048), F32), i...  31.7 us
    unnamed x1, local copies, waits for them, and re-layouts  1.67 us

profile of v5, /device:TPU:2, one launch (start us, length us, event | category | flops | bytes accessed | tf_op | source)
XLA Modules:
  0.0 33.3 jit_solution(17229681179318008908)
XLA Ops:
  0.0 31.7 %shard_map.127 = f32[32,2048]{1,0:T(8,128)} custom-call(f32[32,2048]{1,0:T(8,128)} %rs.1, f32[3,2048]{1,0:T(4,128)} %pts_in.1, f32[512,256]{1,0:T(8,128)} %bitcast.12, f32[960,64]{1,0:T(8,128)} %bitcast.13, f32[3,15,64]{2,1,0:T(8,128)} %bitcast.15, s32[8,8]{1,0:T(8,128)} %near_list_in.1, s32[8]{0:T(128)} %near_count_in.1, s32[8,15]{1,0:T(8,128)} %bitcast.17, ...), custom_call_target="tpu_custom_call" | custom-call | tf_op jit(solution)/shard_map/pallas_call | solution.py:584
  31.7 1.7 %copy.15 = f32[32,2048]{1,0:T(8,128)} copy(f32[32,2048]{1,0:T(8,128)} %shard_map.127) | data formatting | bytes 524288

commit v6 on v5

--- a/solution.py
+++ b/solution.py
@@ -533,10 +533,10 @@
         group_copy(k, False).wait_recv()
     level2 = [jnp.where(low32, tc[0], tc[1]), jnp.where(low32, tc[2], tc[3])]
     level1 = lift(level2, bu_h, bu_l, 1280)
+    incoming.append(path_field(5, jnp.concatenate(level2, axis=1)))
+    incoming.append(path_field(6, level1))
     for k in range(1, 4):
         plane_copy(k, False).wait_recv()
-    incoming.append(path_field(5, jnp.concatenate(level2, axis=1)))
-    incoming.append(path_field(6, level1))
     incoming.append(path_field(0, group_lanes(0, 512)()))
     incoming.append(path_field(1, group_lanes(512, 768)()))
     incoming.append(path_field(2, group_lanes(768, 896)()))

time: 33.4 us -> 33.6 us (level)
  no operation moved by 1% of the time
where the time goes in v6:
time: 33.6 us; the launch traced here: 33.5 us
  Pallas kernels  31.8 us (95%)
  local copies, waits for them, and re-layouts  1.67 us (5%)
    pallas_call x1, Pallas kernels, on_device(): pl.pallas_call(kernel, out_shape=jax.ShapeDtypeStruct((32, 2048), F32), i...  31.8 us
    unnamed x1, local copies, waits for them, and re-layouts  1.67 us

profile of v6, /device:TPU:2, one launch (start us, length us, event | category | flops | bytes accessed | tf_op | source)
XLA Modules:
  0.0 33.5 jit_solution(7105985764109633904)
XLA Ops:
  0.0 31.8 %shard_map.127 = f32[32,2048]{1,0:T(8,128)} custom-call(f32[32,2048]{1,0:T(8,128)} %rs.1, f32[3,2048]{1,0:T(4,128)} %pts_in.1, f32[512,256]{1,0:T(8,128)} %bitcast.12, f32[960,64]{1,0:T(8,128)} %bitcast.13, f32[3,15,64]{2,1,0:T(8,128)} %bitcast.15, s32[8,8]{1,0:T(8,128)} %near_list_in.1, s32[8]{0:T(128)} %near_count_in.1, s32[8,15]{1,0:T(8,128)} %bitcast.17, ...), custom_call_target="tpu_custom_call" | custom-call | tf_op jit(solution)/shard_map/pallas_call | solution.py:584
  31.8 1.7 %copy.15 = f32[32,2048]{1,0:T(8,128)} copy(f32[32,2048]{1,0:T(8,128)} %shard_map.127) | data formatting | bytes 524288
